TPU v7x, 32 devices: a whole 2x2x4 slice. The times are simulated.
32 devices in a mesh: section: 2 (over x), lat: 4 (over y, core), lon: 4 (over z).
Axes of the slice: x: 2, y: 2, z: 4, core: 2. Of those that a mesh axis runs over, the one named last changes fastest.
Arguments:
- start: bfloat16 [2, 12, 32, 1024], P('section', None, 'lat', 'lon'), may hold values from -6 to 6
- prior_mean: bfloat16 [12, 32, 1024], P(None, 'lat', 'lon'), may hold values from -6 to 6
- lift_w: bfloat16 [2, 24, 128], P('section'), may hold values from -1.25 to 1.25
- noise_gain: float32 [2, 128], P('section'), may hold values from -8 to 8
- conv0a: bfloat16 [2, 9, 128, 128], P('section'), may hold values from -0.25 to 0.25
- expand: bfloat16 [2, 128, 256], P('section'), may hold values from -0.5 to 0.5
- conv1a: bfloat16 [2, 9, 256, 256], P('section'), may hold values from -0.1875 to 0.1875
- conv1b: bfloat16 [2, 9, 256, 256], P('section'), may hold values from -0.1875 to 0.1875
- shrink: bfloat16 [2, 256, 128], P('section'), may hold values from -0.375 to 0.375
- conv0b: bfloat16 [2, 9, 128, 128], P('section'), may hold values from -0.25 to 0.25
- head: bfloat16 [2, 128, 12], P('section'), may hold values from -0.5 to 0.5
Outputs:
- results: bfloat16 [2, 12, 32, 1024], P('section', None, 'lat', 'lon')
All inputs are finite; a program needn't handle non-finite values.
Results may differ from a plain program's by a relative error of at most 0.013.
Values may be sent and summed in bfloat16 or wider, within the bound.
A program may use at most 64 MiB of HBM per device.

v0:
```python
import math

import jax
import jax.numpy as jnp
from jax import lax
from jax.sharding import PartitionSpec as P

sigma_data = 0.5
sigma_high = 2.0
sigma_low = 0.5


def extended(x, sides, width):
    for axis, dim in sides:
        size, length = (lax.axis_size(axis), x.shape[dim])
        up = [(i, (i + 1) % size) for i in range(size)]
        down = [(j, i) for i, j in up]
        last = lax.slice_in_dim(x, length - width, length, axis=dim)
        first = lax.slice_in_dim(x, 0, width, axis=dim)
        before = lax.ppermute(last, axis, up)
        after = lax.ppermute(first, axis, down)
        x = jnp.concatenate([before, x, after], axis=dim)
    return x


def swapped(value, axis, apart):
    mask = 2**apart
    pairs = [(source, source ^ mask) for source in range(lax.axis_size(axis))]
    return lax.ppermute(value, axis, pairs)


def precondition(sigma):
    total = sigma * sigma + sigma_data * sigma_data
    return (
        1.0 / math.sqrt(total),
        sigma_data * sigma_data / total,
        sigma * sigma_data / math.sqrt(total),
        math.log(sigma) / 4.0,
    )


def band_edges(field, depth, axis):
    count = field.shape[axis]
    position = lax.axis_index("lat")
    final = lax.axis_size("lat") - 1
    places = jnp.arange(count)
    outside = (places < depth) & (position == 0) | (places >= count - depth) & (position == final)
    layout = [1] * field.ndim
    layout[axis] = count
    return jnp.where(outside.reshape(layout), jnp.zeros((), field.dtype), field)


def convolve(padded, kernel, height, breadth):
    channels = padded.shape[-1]
    total = jnp.zeros((height * breadth, kernel.shape[-1]), jnp.float32)
    for offset in range(9):
        down, across = divmod(offset, 3)
        window = padded[down : down + height, across : across + breadth].reshape(
            height * breadth, channels
        )
        total = total + jnp.dot(window, kernel[offset], preferred_element_type=jnp.float32)
    return total.reshape(height, breadth, -1)


def lift(fields, lift_w, shift):
    channels, height, breadth = fields.shape
    flat = fields.reshape(channels, height * breadth)
    hidden = lax.dot_general(
        flat, lift_w, (((0,), (0,)), ((), ())), preferred_element_type=jnp.float32
    )
    return jax.nn.silu(hidden + shift).astype(jnp.bfloat16).reshape(height, breadth, -1)


def wide_rim(field):
    return band_edges(extended(field, (("lat", 0), ("lon", 1)), 1), 1, 0)


def coarse_rim(field):
    return band_edges(extended(field, (("lat", 0), ("lon", 1)), 1), 1, 0)


def network(state, prior, shift, weights):
    lift_w, conv0a, expand, conv1a, conv1b, shrink, conv0b, head = weights
    fields = jnp.concatenate([state, prior], axis=0)
    height = state.shape[1]
    breadth = state.shape[2]
    padded = wide_rim(lift(fields, lift_w, shift))
    first_level = jax.nn.silu(convolve(padded, conv0a, height, breadth)).astype(jnp.bfloat16)
    half_h = height // 2
    half_b = breadth // 2
    pooled = (
        jnp.sum(first_level.reshape(half_h, 2, half_b, 2, -1), axis=(1, 3), dtype=jnp.float32)
        * 0.25
    ).astype(jnp.bfloat16)
    widened = (
        jnp.dot(pooled.reshape(half_h * half_b, -1), expand, preferred_element_type=jnp.float32)
        .astype(jnp.bfloat16)
        .reshape(half_h, half_b, -1)
    )
    inner = jax.nn.silu(convolve(coarse_rim(widened), conv1a, half_h, half_b)).astype(jnp.bfloat16)
    inner = coarse_rim(inner)
    coarse_out = (
        jax.nn.silu(convolve(inner, conv1b, half_h, half_b)) + widened.astype(jnp.float32)
    ).astype(jnp.bfloat16)
    projected = jnp.dot(
        coarse_out.reshape(half_h * half_b, -1), shrink, preferred_element_type=jnp.float32
    ).reshape(half_h, 1, half_b, 1, -1)
    spread = jnp.broadcast_to(projected, (half_h, 2, half_b, 2, projected.shape[-1])).reshape(
        height, breadth, -1
    )
    merged = (spread + first_level.astype(jnp.float32)).astype(jnp.bfloat16)
    last_level = jax.nn.silu(convolve(wide_rim(merged), conv0b, height, breadth)).astype(
        jnp.bfloat16
    )
    output = lax.dot_general(
        head,
        last_level.reshape(height * breadth, -1),
        (((0,), (1,)), ((), ())),
        preferred_element_type=jnp.float32,
    )
    return output.reshape(-1, height, breadth)


def on_device(
    start, prior_mean, lift_w, noise_gain, conv0a, expand, conv1a, conv1b, shrink, conv0b, head
):
    diffuse = lax.axis_index("section") == 1
    weights = (lift_w[0], conv0a[0], expand[0], conv1a[0], conv1b[0], shrink[0], conv0b[0], head[0])
    gain = noise_gain[0]
    high = precondition(sigma_high)
    low = precondition(sigma_low)
    given = start[0].astype(jnp.float32)
    noisy = sigma_high * given
    state = jnp.where(diffuse, high[0] * noisy, given).astype(jnp.bfloat16)
    first_out = network(state, prior_mean, jnp.where(diffuse, high[3], 0.0) * gain, weights)
    first_denoised = high[1] * noisy + high[2] * first_out
    moved = noisy + (sigma_low - sigma_high) / sigma_high * (noisy - first_denoised)
    second_input = (low[0] * moved).astype(jnp.bfloat16)
    second_out = network(second_input, prior_mean, low[3] * gain, weights)
    second_denoised = low[1] * moved + low[2] * second_out
    sample = (prior_mean.astype(jnp.float32) + second_denoised).astype(jnp.bfloat16)
    outgoing = jnp.where(diffuse, sample, first_out.astype(jnp.bfloat16))
    arrived = swapped(outgoing, "section", 0)
    return arrived[None]


def solution(mesh):
    placed = (
        P("section", None, "lat", "lon"),
        P(None, "lat", "lon"),
        P("section", None, None),
        P("section", None),
        P("section", None, None, None),
        P("section", None, None),
        P("section", None, None, None),
        P("section", None, None, None),
        P("section", None, None),
        P("section", None, None, None),
        P("section", None, None),
    )
    return jax.shard_map(
        on_device,
        mesh=mesh,
        in_specs=placed,
        out_specs=P("section", None, "lat", "lon"),
        check_vma=False,
    )
```

profile of v0, /device:TPU:0, one launch (start us, length us, event | category | flops | bytes accessed | tf_op | source)
XLA Modules:
  0.0 125.5 jit_solution(6290325395052131406)
XLA Ops:
  4.1 2.0 %collective-permute-start.1 = (bf16[1,256,128]{2,1,0:T(8,128)(2,1)S(1)}, bf16[1,256,128]{2,1,0:T(8,128)(2,1)S(1)}, u32[]{:S(2)}, u32[]{:S(2)}) collective-permute-start(bf16[1,256,128]{2,1,0:T(8,128)(2,1)S(1)} %get-tuple-element.56), channel_id=1, source_target_pairs={{4,0},{8,4},{12,8},{0,12},{5,1},{9,5},{13,9},{1,13},{6,2},{10,6},{... | collective-permute-start | bytes 196616 | tf_op jit(solution)/shard_map/ppermute | solution.py:21
  6.1 1.9 %collective-permute-done = bf16[1,256,128]{2,1,0:T(8,128)(2,1)S(1)} collective-permute-done((bf16[1,256,128]{2,1,0:T(8,128)(2,1)S(1)}, bf16[1,256,128]{2,1,0:T(8,128)(2,1)S(1)}, u32[]{:S(2)}, u32[]{:S(2)}) %collective-permute-start) | collective-permute-done | bytes 65568 | tf_op jit(solution)/shard_map/ppermute | solution.py:20
  8.5 1.9 %collective-permute-start.2 = (bf16[10,1,128]{2,1,0:T(2,128)(2,1)S(1)}, bf16[10,1,128]{2,1,0:T(2,128)(2,1)S(1)}, u32[]{:S(2)}, u32[]{:S(2)}) collective-permute-start(bf16[10,1,128]{2,1,0:T(2,128)(2,1)S(1)} %get-tuple-element.47), channel_id=1, source_target_pairs={{0,1},{1,2},{2,3},{3,0},{4,5},{5,6},{6,7},{7,4},{8,9},{9,10},{10,1... | collective-permute-start | bytes 7688 | tf_op jit(solution)/shard_map/ppermute | solution.py:20
  10.4 2.1 %collective-permute-start.3 = (bf16[10,1,128]{2,1,0:T(2,128)(2,1)S(1)}, bf16[10,1,128]{2,1,0:T(2,128)(2,1)S(1)}, u32[]{:S(2)}, u32[]{:S(2)}) collective-permute-start(bf16[10,1,128]{2,1,0:T(2,128)(2,1)S(1)} %get-tuple-element.48), channel_id=1, source_target_pairs={{1,0},{2,1},{3,2},{0,3},{5,4},{6,5},{7,6},{4,7},{9,8},{10,9},{11,1... | collective-permute-start | bytes 7688 | tf_op jit(solution)/shard_map/ppermute | solution.py:21
  12.5 1.6 %collective-permute-done.2 = bf16[10,1,128]{2,1,0:T(2,128)(2,1)S(1)} collective-permute-done((bf16[10,1,128]{2,1,0:T(2,128)(2,1)S(1)}, bf16[10,1,128]{2,1,0:T(2,128)(2,1)S(1)}, u32[]{:S(2)}, u32[]{:S(2)}) %collective-permute-start.2) | collective-permute-done | bytes 2592 | tf_op jit(solution)/shard_map/ppermute | solution.py:20
  20.3 1.9 %collective-permute-done.4 = bf16[1,128,256]{2,1,0:T(8,128)(2,1)S(1)} collective-permute-done((bf16[1,128,256]{2,1,0:T(8,128)(2,1)S(1)}, bf16[1,128,256]{2,1,0:T(8,128)(2,1)S(1)}, u32[]{:S(2)}, u32[]{:S(2)}) %collective-permute-start.4) | collective-permute-done | bytes 65568 | tf_op jit(solution)/shard_map/ppermute | solution.py:20
  23.8 2.9 %collective-permute-start.7 = (bf16[6,1,256]{2,1,0:T(2,128)(2,1)S(1)}, bf16[6,1,256]{2,1,0:T(2,128)(2,1)S(1)}, u32[]{:S(2)}, u32[]{:S(2)}) collective-permute-start(bf16[6,1,256]{2,1,0:T(2,128)(2,1)S(1)} %get-tuple-element.100), channel_id=1, source_target_pairs={{1,0},{2,1},{3,2},{0,3},{5,4},{6,5},{7,6},{4,7},{9,8},{10,9},{11,1... | collective-permute-start | bytes 9224 | tf_op jit(solution)/shard_map/ppermute | solution.py:21
  26.7 1.5 %collective-permute-done.6 = bf16[6,1,256]{2,1,0:T(2,128)(2,1)S(1)} collective-permute-done((bf16[6,1,256]{2,1,0:T(2,128)(2,1)S(1)}, bf16[6,1,256]{2,1,0:T(2,128)(2,1)S(1)}, u32[]{:S(2)}, u32[]{:S(2)}) %collective-permute-start.6) | collective-permute-done | bytes 3104 | tf_op jit(solution)/shard_map/ppermute | solution.py:20
  33.8 1.9 %collective-permute-done.8 = bf16[1,128,256]{2,1,0:T(8,128)(2,1)S(1)} collective-permute-done((bf16[1,128,256]{2,1,0:T(8,128)(2,1)S(1)}, bf16[1,128,256]{2,1,0:T(8,128)(2,1)S(1)}, u32[]{:S(2)}, u32[]{:S(2)}) %collective-permute-start.8) | collective-permute-done | bytes 65568 | tf_op jit(solution)/shard_map/ppermute | solution.py:20
  37.4 2.8 %collective-permute-start.11 = (bf16[6,1,256]{2,1,0:T(2,128)(2,1)S(1)}, bf16[6,1,256]{2,1,0:T(2,128)(2,1)S(1)}, u32[]{:S(2)}, u32[]{:S(2)}) collective-permute-start(bf16[6,1,256]{2,1,0:T(2,128)(2,1)S(1)} %get-tuple-element.98), channel_id=1, source_target_pairs={{1,0},{2,1},{3,2},{0,3},{5,4},{6,5},{7,6},{4,7},{9,8},{10,9},{11,1... | collective-permute-start | bytes 9224 | tf_op jit(solution)/shard_map/ppermute | solution.py:21
  40.2 1.5 %collective-permute-done.10 = bf16[6,1,256]{2,1,0:T(2,128)(2,1)S(1)} collective-permute-done((bf16[6,1,256]{2,1,0:T(2,128)(2,1)S(1)}, bf16[6,1,256]{2,1,0:T(2,128)(2,1)S(1)}, u32[]{:S(2)}, u32[]{:S(2)}) %collective-permute-start.10) | collective-permute-done | bytes 3104 | tf_op jit(solution)/shard_map/ppermute | solution.py:20
  48.6 1.9 %collective-permute-done.12 = bf16[1,256,128]{2,1,0:T(8,128)(2,1)S(1)} collective-permute-done((bf16[1,256,128]{2,1,0:T(8,128)(2,1)S(1)}, bf16[1,256,128]{2,1,0:T(8,128)(2,1)S(1)}, u32[]{:S(2)}, u32[]{:S(2)}) %collective-permute-start.12) | collective-permute-done | bytes 65568 | tf_op jit(solution)/shard_map/ppermute | solution.py:20
  52.1 2.8 %collective-permute-start.15 = (bf16[10,1,128]{2,1,0:T(2,128)(2,1)S(1)}, bf16[10,1,128]{2,1,0:T(2,128)(2,1)S(1)}, u32[]{:S(2)}, u32[]{:S(2)}) collective-permute-start(bf16[10,1,128]{2,1,0:T(2,128)(2,1)S(1)} %get-tuple-element.46), channel_id=1, source_target_pairs={{1,0},{2,1},{3,2},{0,3},{5,4},{6,5},{7,6},{4,7},{9,8},{10,9},{11,1... | collective-permute-start | bytes 7688 | tf_op jit(solution)/shard_map/ppermute | solution.py:21
  60.9 2.5 %fusion.191 = (bf16[2048,12]{0,1:T(8,128)(2,1)}, f32[2048,12]{0,1:T(8,128)}) fusion(bf16[1,128,12]{1,2,0:T(8,128)(2,1)S(1)} %copy-done.10, f32[2048,128]{1,0:T(8,128)} %convolution_add_fusion.18, bf16[2048,128]{1,0:T(8,128)(2,1)S(1)} %bitcast.504, bf16[1,9,128,128]{3,2,1,0:T(8,128)(2,1)S(1)} %copy-done.4), kind=kOutput, calls=%fused_computation.327 | convolution fusion | flops 75022336 | bytes 1757184 | tf_op jit(solution)/shard_map/dot_general | solution.py:115
  67.2 1.7 %collective-permute-start.16 = (bf16[1,256,128]{2,1,0:T(8,128)(2,1)S(1)}, bf16[1,256,128]{2,1,0:T(8,128)(2,1)S(1)}, u32[]{:S(2)}, u32[]{:S(2)}) collective-permute-start(bf16[1,256,128]{2,1,0:T(8,128)(2,1)S(1)} %get-tuple-element.51), channel_id=1, source_target_pairs={{0,4},{4,8},{8,12},{12,0},{1,5},{5,9},{9,13},{13,1},{2,6},{6,10},{... | collective-permute-start | bytes 196616 | tf_op jit(solution)/shard_map/ppermute | solution.py:20
  69.0 1.9 %collective-permute-done.16 = bf16[1,256,128]{2,1,0:T(8,128)(2,1)S(1)} collective-permute-done((bf16[1,256,128]{2,1,0:T(8,128)(2,1)S(1)}, bf16[1,256,128]{2,1,0:T(8,128)(2,1)S(1)}, u32[]{:S(2)}, u32[]{:S(2)}) %collective-permute-start.16) | collective-permute-done | bytes 65568 | tf_op jit(solution)/shard_map/ppermute | solution.py:20
  71.1 1.4 %collective-permute-start.18 = (bf16[10,1,128]{2,1,0:T(2,128)(2,1)S(1)}, bf16[10,1,128]{2,1,0:T(2,128)(2,1)S(1)}, u32[]{:S(2)}, u32[]{:S(2)}) collective-permute-start(bf16[10,1,128]{2,1,0:T(2,128)(2,1)S(1)} %get-tuple-element.43), channel_id=1, source_target_pairs={{0,1},{1,2},{2,3},{3,0},{4,5},{5,6},{6,7},{7,4},{8,9},{9,10},{10,1... | collective-permute-start | bytes 7688 | tf_op jit(solution)/shard_map/ppermute | solution.py:20
  72.5 2.8 %collective-permute-start.19 = (bf16[10,1,128]{2,1,0:T(2,128)(2,1)S(1)}, bf16[10,1,128]{2,1,0:T(2,128)(2,1)S(1)}, u32[]{:S(2)}, u32[]{:S(2)}) collective-permute-start(bf16[10,1,128]{2,1,0:T(2,128)(2,1)S(1)} %get-tuple-element.44), channel_id=1, source_target_pairs={{1,0},{2,1},{3,2},{0,3},{5,4},{6,5},{7,6},{4,7},{9,8},{10,9},{11,1... | collective-permute-start | bytes 7688 | tf_op jit(solution)/shard_map/ppermute | solution.py:21
  75.3 1.5 %collective-permute-done.18 = bf16[10,1,128]{2,1,0:T(2,128)(2,1)S(1)} collective-permute-done((bf16[10,1,128]{2,1,0:T(2,128)(2,1)S(1)}, bf16[10,1,128]{2,1,0:T(2,128)(2,1)S(1)}, u32[]{:S(2)}, u32[]{:S(2)}) %collective-permute-start.18) | collective-permute-done | bytes 2592 | tf_op jit(solution)/shard_map/ppermute | solution.py:20
  81.2 2.0 %collective-permute-start.20 = (bf16[1,128,256]{2,1,0:T(8,128)(2,1)S(1)}, bf16[1,128,256]{2,1,0:T(8,128)(2,1)S(1)}, u32[]{:S(2)}, u32[]{:S(2)}) collective-permute-start(bf16[1,128,256]{2,1,0:T(8,128)(2,1)S(1)} %get-tuple-element.103), channel_id=1, source_target_pairs={{0,4},{4,8},{8,12},{12,0},{1,5},{5,9},{9,13},{13,1},{2,6},{6,10},{... | collective-permute-start | bytes 196616 | tf_op jit(solution)/shard_map/ppermute | solution.py:20
  83.1 1.8 %collective-permute-done.20 = bf16[1,128,256]{2,1,0:T(8,128)(2,1)S(1)} collective-permute-done((bf16[1,128,256]{2,1,0:T(8,128)(2,1)S(1)}, bf16[1,128,256]{2,1,0:T(8,128)(2,1)S(1)}, u32[]{:S(2)}, u32[]{:S(2)}) %collective-permute-start.20) | collective-permute-done | bytes 65568 | tf_op jit(solution)/shard_map/ppermute | solution.py:20
  86.2 3.0 %collective-permute-start.23 = (bf16[6,1,256]{2,1,0:T(2,128)(2,1)S(1)}, bf16[6,1,256]{2,1,0:T(2,128)(2,1)S(1)}, u32[]{:S(2)}, u32[]{:S(2)}) collective-permute-start(bf16[6,1,256]{2,1,0:T(2,128)(2,1)S(1)} %get-tuple-element.96), channel_id=1, source_target_pairs={{1,0},{2,1},{3,2},{0,3},{5,4},{6,5},{7,6},{4,7},{9,8},{10,9},{11,1... | collective-permute-start | bytes 9224 | tf_op jit(solution)/shard_map/ppermute | solution.py:21
  89.2 1.6 %collective-permute-done.22 = bf16[6,1,256]{2,1,0:T(2,128)(2,1)S(1)} collective-permute-done((bf16[6,1,256]{2,1,0:T(2,128)(2,1)S(1)}, bf16[6,1,256]{2,1,0:T(2,128)(2,1)S(1)}, u32[]{:S(2)}, u32[]{:S(2)}) %collective-permute-start.22) | collective-permute-done | bytes 3104 | tf_op jit(solution)/shard_map/ppermute | solution.py:20
  93.6 1.8 %collective-permute-start.24 = (bf16[1,128,256]{2,1,0:T(8,128)(2,1)S(1)}, bf16[1,128,256]{2,1,0:T(8,128)(2,1)S(1)}, u32[]{:S(2)}, u32[]{:S(2)}) collective-permute-start(bf16[1,128,256]{2,1,0:T(8,128)(2,1)S(1)} %get-tuple-element.101), channel_id=1, source_target_pairs={{0,4},{4,8},{8,12},{12,0},{1,5},{5,9},{9,13},{13,1},{2,6},{6,10},{... | collective-permute-start | bytes 196616 | tf_op jit(solution)/shard_map/ppermute | solution.py:20
  95.5 1.9 %collective-permute-done.24 = bf16[1,128,256]{2,1,0:T(8,128)(2,1)S(1)} collective-permute-done((bf16[1,128,256]{2,1,0:T(8,128)(2,1)S(1)}, bf16[1,128,256]{2,1,0:T(8,128)(2,1)S(1)}, u32[]{:S(2)}, u32[]{:S(2)}) %collective-permute-start.24) | collective-permute-done | bytes 65568 | tf_op jit(solution)/shard_map/ppermute | solution.py:20
  98.6 2.9 %collective-permute-start.27 = (bf16[6,1,256]{2,1,0:T(2,128)(2,1)S(1)}, bf16[6,1,256]{2,1,0:T(2,128)(2,1)S(1)}, u32[]{:S(2)}, u32[]{:S(2)}) collective-permute-start(bf16[6,1,256]{2,1,0:T(2,128)(2,1)S(1)} %get-tuple-element.94), channel_id=1, source_target_pairs={{1,0},{2,1},{3,2},{0,3},{5,4},{6,5},{7,6},{4,7},{9,8},{10,9},{11,1... | collective-permute-start | bytes 9224 | tf_op jit(solution)/shard_map/ppermute | solution.py:21
  101.5 1.6 %collective-permute-done.26 = bf16[6,1,256]{2,1,0:T(2,128)(2,1)S(1)} collective-permute-done((bf16[6,1,256]{2,1,0:T(2,128)(2,1)S(1)}, bf16[6,1,256]{2,1,0:T(2,128)(2,1)S(1)}, u32[]{:S(2)}, u32[]{:S(2)}) %collective-permute-start.26) | collective-permute-done | bytes 3104 | tf_op jit(solution)/shard_map/ppermute | solution.py:20
  107.2 1.8 %collective-permute-start.28 = (bf16[1,256,128]{2,1,0:T(8,128)(2,1)S(1)}, bf16[1,256,128]{2,1,0:T(8,128)(2,1)S(1)}, u32[]{:S(2)}, u32[]{:S(2)}) collective-permute-start(bf16[1,256,128]{2,1,0:T(8,128)(2,1)S(1)} %get-tuple-element.49), channel_id=1, source_target_pairs={{0,4},{4,8},{8,12},{12,0},{1,5},{5,9},{9,13},{13,1},{2,6},{6,10},{... | collective-permute-start | bytes 196616 | tf_op jit(solution)/shard_map/ppermute | solution.py:20
  109.0 1.9 %collective-permute-done.28 = bf16[1,256,128]{2,1,0:T(8,128)(2,1)S(1)} collective-permute-done((bf16[1,256,128]{2,1,0:T(8,128)(2,1)S(1)}, bf16[1,256,128]{2,1,0:T(8,128)(2,1)S(1)}, u32[]{:S(2)}, u32[]{:S(2)}) %collective-permute-start.28) | collective-permute-done | bytes 65568 | tf_op jit(solution)/shard_map/ppermute | solution.py:20
  112.0 3.1 %collective-permute-start.31 = (bf16[10,1,128]{2,1,0:T(2,128)(2,1)S(1)}, bf16[10,1,128]{2,1,0:T(2,128)(2,1)S(1)}, u32[]{:S(2)}, u32[]{:S(2)}) collective-permute-start(bf16[10,1,128]{2,1,0:T(2,128)(2,1)S(1)} %get-tuple-element.42), channel_id=1, source_target_pairs={{1,0},{2,1},{3,2},{0,3},{5,4},{6,5},{7,6},{4,7},{9,8},{10,9},{11,1... | collective-permute-start | bytes 7688 | tf_op jit(solution)/shard_map/ppermute | solution.py:21
  115.2 1.4 %collective-permute-done.30 = bf16[10,1,128]{2,1,0:T(2,128)(2,1)S(1)} collective-permute-done((bf16[10,1,128]{2,1,0:T(2,128)(2,1)S(1)}, bf16[10,1,128]{2,1,0:T(2,128)(2,1)S(1)}, u32[]{:S(2)}, u32[]{:S(2)}) %collective-permute-start.30) | collective-permute-done | bytes 2592 | tf_op jit(solution)/shard_map/ppermute | solution.py:20
  120.8 4.1 %collective-permute-done.32 = bf16[12,8,256]{2,1,0:T(8,128)(2,1)S(1)} collective-permute-done((bf16[12,8,256]{2,1,0:T(8,128)(2,1)S(1)}, bf16[12,8,256]{2,1,0:T(8,128)(2,1)S(1)}, u32[]{:S(2)}, u32[]{:S(2)}) %collective-permute-start.32) | collective-permute-done | bytes 49184 | tf_op jit(solution)/shard_map/ppermute | solution.py:29
  (190 shorter events, 56.8 us)
Async XLA Ops:
  3.6 4.4 %collective-permute-start = (bf16[1,256,128]{2,1,0:T(8,128)(2,1)S(1)}, bf16[1,256,128]{2,1,0:T(8,128)(2,1)S(1)}, u32[]{:S(2)}, u32[]{:S(2)}) collective-permute-start(bf16[1,256,128]{2,1,0:T(8,128)(2,1)S(1)} %get-tuple-element.55), channel_id=1, source_target_pairs={{0,4},{4,8},{8,12},{12,0},{1,5},{5,9},{9,13},{13,1},{2,6},{6,10},{... | collective-permute-start | bytes 196616 | tf_op jit(solution)/shard_map/ppermute | solution.py:20
  4.1 4.4 %collective-permute-start.1 = (bf16[1,256,128]{2,1,0:T(8,128)(2,1)S(1)}, bf16[1,256,128]{2,1,0:T(8,128)(2,1)S(1)}, u32[]{:S(2)}, u32[]{:S(2)}) collective-permute-start(bf16[1,256,128]{2,1,0:T(8,128)(2,1)S(1)} %get-tuple-element.56), channel_id=1, source_target_pairs={{4,0},{8,4},{12,8},{0,12},{5,1},{9,5},{13,9},{1,13},{6,2},{10,6},{... | collective-permute-start | bytes 196616 | tf_op jit(solution)/shard_map/ppermute | solution.py:21
  8.5 5.6 %collective-permute-start.2 = (bf16[10,1,128]{2,1,0:T(2,128)(2,1)S(1)}, bf16[10,1,128]{2,1,0:T(2,128)(2,1)S(1)}, u32[]{:S(2)}, u32[]{:S(2)}) collective-permute-start(bf16[10,1,128]{2,1,0:T(2,128)(2,1)S(1)} %get-tuple-element.47), channel_id=1, source_target_pairs={{0,1},{1,2},{2,3},{3,0},{4,5},{5,6},{6,7},{7,4},{8,9},{9,10},{10,1... | collective-permute-start | bytes 7688 | tf_op jit(solution)/shard_map/ppermute | solution.py:20
  10.4 3.7 %collective-permute-start.3 = (bf16[10,1,128]{2,1,0:T(2,128)(2,1)S(1)}, bf16[10,1,128]{2,1,0:T(2,128)(2,1)S(1)}, u32[]{:S(2)}, u32[]{:S(2)}) collective-permute-start(bf16[10,1,128]{2,1,0:T(2,128)(2,1)S(1)} %get-tuple-element.48), channel_id=1, source_target_pairs={{1,0},{2,1},{3,2},{0,3},{5,4},{6,5},{7,6},{4,7},{9,8},{10,9},{11,1... | collective-permute-start | bytes 7688 | tf_op jit(solution)/shard_map/ppermute | solution.py:21
  18.5 3.7 %collective-permute-start.4 = (bf16[1,128,256]{2,1,0:T(8,128)(2,1)S(1)}, bf16[1,128,256]{2,1,0:T(8,128)(2,1)S(1)}, u32[]{:S(2)}, u32[]{:S(2)}) collective-permute-start(bf16[1,128,256]{2,1,0:T(8,128)(2,1)S(1)} %get-tuple-element.107), channel_id=1, source_target_pairs={{0,4},{4,8},{8,12},{12,0},{1,5},{5,9},{9,13},{13,1},{2,6},{6,10},{... | collective-permute-start | bytes 196616 | tf_op jit(solution)/shard_map/ppermute | solution.py:20
  19.2 3.5 %collective-permute-start.5 = (bf16[1,128,256]{2,1,0:T(8,128)(2,1)S(1)}, bf16[1,128,256]{2,1,0:T(8,128)(2,1)S(1)}, u32[]{:S(2)}, u32[]{:S(2)}) collective-permute-start(bf16[1,128,256]{2,1,0:T(8,128)(2,1)S(1)} %get-tuple-element.108), channel_id=1, source_target_pairs={{4,0},{8,4},{12,8},{0,12},{5,1},{9,5},{13,9},{1,13},{6,2},{10,6},{... | collective-permute-start | bytes 196616 | tf_op jit(solution)/shard_map/ppermute | solution.py:21
  22.8 5.5 %collective-permute-start.6 = (bf16[6,1,256]{2,1,0:T(2,128)(2,1)S(1)}, bf16[6,1,256]{2,1,0:T(2,128)(2,1)S(1)}, u32[]{:S(2)}, u32[]{:S(2)}) collective-permute-start(bf16[6,1,256]{2,1,0:T(2,128)(2,1)S(1)} %get-tuple-element.99), channel_id=1, source_target_pairs={{0,1},{1,2},{2,3},{3,0},{4,5},{5,6},{6,7},{7,4},{8,9},{9,10},{10,1... | collective-permute-start | bytes 9224 | tf_op jit(solution)/shard_map/ppermute | solution.py:20
  23.8 4.5 %collective-permute-start.7 = (bf16[6,1,256]{2,1,0:T(2,128)(2,1)S(1)}, bf16[6,1,256]{2,1,0:T(2,128)(2,1)S(1)}, u32[]{:S(2)}, u32[]{:S(2)}) collective-permute-start(bf16[6,1,256]{2,1,0:T(2,128)(2,1)S(1)} %get-tuple-element.100), channel_id=1, source_target_pairs={{1,0},{2,1},{3,2},{0,3},{5,4},{6,5},{7,6},{4,7},{9,8},{10,9},{11,1... | collective-permute-start | bytes 9224 | tf_op jit(solution)/shard_map/ppermute | solution.py:21
  32.0 3.7 %collective-permute-start.8 = (bf16[1,128,256]{2,1,0:T(8,128)(2,1)S(1)}, bf16[1,128,256]{2,1,0:T(8,128)(2,1)S(1)}, u32[]{:S(2)}, u32[]{:S(2)}) collective-permute-start(bf16[1,128,256]{2,1,0:T(8,128)(2,1)S(1)} %get-tuple-element.105), channel_id=1, source_target_pairs={{0,4},{4,8},{8,12},{12,0},{1,5},{5,9},{9,13},{13,1},{2,6},{6,10},{... | collective-permute-start | bytes 196616 | tf_op jit(solution)/shard_map/ppermute | solution.py:20
  33.1 3.1 %collective-permute-start.9 = (bf16[1,128,256]{2,1,0:T(8,128)(2,1)S(1)}, bf16[1,128,256]{2,1,0:T(8,128)(2,1)S(1)}, u32[]{:S(2)}, u32[]{:S(2)}) collective-permute-start(bf16[1,128,256]{2,1,0:T(8,128)(2,1)S(1)} %get-tuple-element.106), channel_id=1, source_target_pairs={{4,0},{8,4},{12,8},{0,12},{5,1},{9,5},{13,9},{1,13},{6,2},{10,6},{... | collective-permute-start | bytes 196616 | tf_op jit(solution)/shard_map/ppermute | solution.py:21
  36.2 5.5 %collective-permute-start.10 = (bf16[6,1,256]{2,1,0:T(2,128)(2,1)S(1)}, bf16[6,1,256]{2,1,0:T(2,128)(2,1)S(1)}, u32[]{:S(2)}, u32[]{:S(2)}) collective-permute-start(bf16[6,1,256]{2,1,0:T(2,128)(2,1)S(1)} %get-tuple-element.97), channel_id=1, source_target_pairs={{0,1},{1,2},{2,3},{3,0},{4,5},{5,6},{6,7},{7,4},{8,9},{9,10},{10,1... | collective-permute-start | bytes 9224 | tf_op jit(solution)/shard_map/ppermute | solution.py:20
  37.4 4.4 %collective-permute-start.11 = (bf16[6,1,256]{2,1,0:T(2,128)(2,1)S(1)}, bf16[6,1,256]{2,1,0:T(2,128)(2,1)S(1)}, u32[]{:S(2)}, u32[]{:S(2)}) collective-permute-start(bf16[6,1,256]{2,1,0:T(2,128)(2,1)S(1)} %get-tuple-element.98), channel_id=1, source_target_pairs={{1,0},{2,1},{3,2},{0,3},{5,4},{6,5},{7,6},{4,7},{9,8},{10,9},{11,1... | collective-permute-start | bytes 9224 | tf_op jit(solution)/shard_map/ppermute | solution.py:21
  46.8 3.7 %collective-permute-start.12 = (bf16[1,256,128]{2,1,0:T(8,128)(2,1)S(1)}, bf16[1,256,128]{2,1,0:T(8,128)(2,1)S(1)}, u32[]{:S(2)}, u32[]{:S(2)}) collective-permute-start(bf16[1,256,128]{2,1,0:T(8,128)(2,1)S(1)} %get-tuple-element.53), channel_id=1, source_target_pairs={{0,4},{4,8},{8,12},{12,0},{1,5},{5,9},{9,13},{13,1},{2,6},{6,10},{... | collective-permute-start | bytes 196616 | tf_op jit(solution)/shard_map/ppermute | solution.py:20
  48.1 2.7 %collective-permute-start.13 = (bf16[1,256,128]{2,1,0:T(8,128)(2,1)S(1)}, bf16[1,256,128]{2,1,0:T(8,128)(2,1)S(1)}, u32[]{:S(2)}, u32[]{:S(2)}) collective-permute-start(bf16[1,256,128]{2,1,0:T(8,128)(2,1)S(1)} %get-tuple-element.54), channel_id=1, source_target_pairs={{4,0},{8,4},{12,8},{0,12},{5,1},{9,5},{13,9},{1,13},{6,2},{10,6},{... | collective-permute-start | bytes 196616 | tf_op jit(solution)/shard_map/ppermute | solution.py:21
  50.8 5.5 %collective-permute-start.14 = (bf16[10,1,128]{2,1,0:T(2,128)(2,1)S(1)}, bf16[10,1,128]{2,1,0:T(2,128)(2,1)S(1)}, u32[]{:S(2)}, u32[]{:S(2)}) collective-permute-start(bf16[10,1,128]{2,1,0:T(2,128)(2,1)S(1)} %get-tuple-element.45), channel_id=1, source_target_pairs={{0,1},{1,2},{2,3},{3,0},{4,5},{5,6},{6,7},{7,4},{8,9},{9,10},{10,1... | collective-permute-start | bytes 7688 | tf_op jit(solution)/shard_map/ppermute | solution.py:20
  52.1 4.2 %collective-permute-start.15 = (bf16[10,1,128]{2,1,0:T(2,128)(2,1)S(1)}, bf16[10,1,128]{2,1,0:T(2,128)(2,1)S(1)}, u32[]{:S(2)}, u32[]{:S(2)}) collective-permute-start(bf16[10,1,128]{2,1,0:T(2,128)(2,1)S(1)} %get-tuple-element.46), channel_id=1, source_target_pairs={{1,0},{2,1},{3,2},{0,3},{5,4},{6,5},{7,6},{4,7},{9,8},{10,9},{11,1... | collective-permute-start | bytes 7688 | tf_op jit(solution)/shard_map/ppermute | solution.py:21
  67.2 3.7 %collective-permute-start.16 = (bf16[1,256,128]{2,1,0:T(8,128)(2,1)S(1)}, bf16[1,256,128]{2,1,0:T(8,128)(2,1)S(1)}, u32[]{:S(2)}, u32[]{:S(2)}) collective-permute-start(bf16[1,256,128]{2,1,0:T(8,128)(2,1)S(1)} %get-tuple-element.51), channel_id=1, source_target_pairs={{0,4},{4,8},{8,12},{12,0},{1,5},{5,9},{9,13},{13,1},{2,6},{6,10},{... | collective-permute-start | bytes 196616 | tf_op jit(solution)/shard_map/ppermute | solution.py:20
  68.9 2.2 %collective-permute-start.17 = (bf16[1,256,128]{2,1,0:T(8,128)(2,1)S(1)}, bf16[1,256,128]{2,1,0:T(8,128)(2,1)S(1)}, u32[]{:S(2)}, u32[]{:S(2)}) collective-permute-start(bf16[1,256,128]{2,1,0:T(8,128)(2,1)S(1)} %get-tuple-element.52), channel_id=1, source_target_pairs={{4,0},{8,4},{12,8},{0,12},{5,1},{9,5},{13,9},{1,13},{6,2},{10,6},{... | collective-permute-start | bytes 196616 | tf_op jit(solution)/shard_map/ppermute | solution.py:21
  71.1 5.7 %collective-permute-start.18 = (bf16[10,1,128]{2,1,0:T(2,128)(2,1)S(1)}, bf16[10,1,128]{2,1,0:T(2,128)(2,1)S(1)}, u32[]{:S(2)}, u32[]{:S(2)}) collective-permute-start(bf16[10,1,128]{2,1,0:T(2,128)(2,1)S(1)} %get-tuple-element.43), channel_id=1, source_target_pairs={{0,1},{1,2},{2,3},{3,0},{4,5},{5,6},{6,7},{7,4},{8,9},{9,10},{10,1... | collective-permute-start | bytes 7688 | tf_op jit(solution)/shard_map/ppermute | solution.py:20
  72.5 4.4 %collective-permute-start.19 = (bf16[10,1,128]{2,1,0:T(2,128)(2,1)S(1)}, bf16[10,1,128]{2,1,0:T(2,128)(2,1)S(1)}, u32[]{:S(2)}, u32[]{:S(2)}) collective-permute-start(bf16[10,1,128]{2,1,0:T(2,128)(2,1)S(1)} %get-tuple-element.44), channel_id=1, source_target_pairs={{1,0},{2,1},{3,2},{0,3},{5,4},{6,5},{7,6},{4,7},{9,8},{10,9},{11,1... | collective-permute-start | bytes 7688 | tf_op jit(solution)/shard_map/ppermute | solution.py:21
  81.2 3.7 %collective-permute-start.20 = (bf16[1,128,256]{2,1,0:T(8,128)(2,1)S(1)}, bf16[1,128,256]{2,1,0:T(8,128)(2,1)S(1)}, u32[]{:S(2)}, u32[]{:S(2)}) collective-permute-start(bf16[1,128,256]{2,1,0:T(8,128)(2,1)S(1)} %get-tuple-element.103), channel_id=1, source_target_pairs={{0,4},{4,8},{8,12},{12,0},{1,5},{5,9},{9,13},{13,1},{2,6},{6,10},{... | collective-permute-start | bytes 196616 | tf_op jit(solution)/shard_map/ppermute | solution.py:20
  83.1 2.2 %collective-permute-start.21 = (bf16[1,128,256]{2,1,0:T(8,128)(2,1)S(1)}, bf16[1,128,256]{2,1,0:T(8,128)(2,1)S(1)}, u32[]{:S(2)}, u32[]{:S(2)}) collective-permute-start(bf16[1,128,256]{2,1,0:T(8,128)(2,1)S(1)} %get-tuple-element.104), channel_id=1, source_target_pairs={{4,0},{8,4},{12,8},{0,12},{5,1},{9,5},{13,9},{1,13},{6,2},{10,6},{... | collective-permute-start | bytes 196616 | tf_op jit(solution)/shard_map/ppermute | solution.py:21
  85.3 5.5 %collective-permute-start.22 = (bf16[6,1,256]{2,1,0:T(2,128)(2,1)S(1)}, bf16[6,1,256]{2,1,0:T(2,128)(2,1)S(1)}, u32[]{:S(2)}, u32[]{:S(2)}) collective-permute-start(bf16[6,1,256]{2,1,0:T(2,128)(2,1)S(1)} %get-tuple-element.95), channel_id=1, source_target_pairs={{0,1},{1,2},{2,3},{3,0},{4,5},{5,6},{6,7},{7,4},{8,9},{9,10},{10,1... | collective-permute-start | bytes 9224 | tf_op jit(solution)/shard_map/ppermute | solution.py:20
  86.2 4.6 %collective-permute-start.23 = (bf16[6,1,256]{2,1,0:T(2,128)(2,1)S(1)}, bf16[6,1,256]{2,1,0:T(2,128)(2,1)S(1)}, u32[]{:S(2)}, u32[]{:S(2)}) collective-permute-start(bf16[6,1,256]{2,1,0:T(2,128)(2,1)S(1)} %get-tuple-element.96), channel_id=1, source_target_pairs={{1,0},{2,1},{3,2},{0,3},{5,4},{6,5},{7,6},{4,7},{9,8},{10,9},{11,1... | collective-permute-start | bytes 9224 | tf_op jit(solution)/shard_map/ppermute | solution.py:21
  93.6 3.7 %collective-permute-start.24 = (bf16[1,128,256]{2,1,0:T(8,128)(2,1)S(1)}, bf16[1,128,256]{2,1,0:T(8,128)(2,1)S(1)}, u32[]{:S(2)}, u32[]{:S(2)}) collective-permute-start(bf16[1,128,256]{2,1,0:T(8,128)(2,1)S(1)} %get-tuple-element.101), channel_id=1, source_target_pairs={{0,4},{4,8},{8,12},{12,0},{1,5},{5,9},{9,13},{13,1},{2,6},{6,10},{... | collective-permute-start | bytes 196616 | tf_op jit(solution)/shard_map/ppermute | solution.py:20
  95.5 2.1 %collective-permute-start.25 = (bf16[1,128,256]{2,1,0:T(8,128)(2,1)S(1)}, bf16[1,128,256]{2,1,0:T(8,128)(2,1)S(1)}, u32[]{:S(2)}, u32[]{:S(2)}) collective-permute-start(bf16[1,128,256]{2,1,0:T(8,128)(2,1)S(1)} %get-tuple-element.102), channel_id=1, source_target_pairs={{4,0},{8,4},{12,8},{0,12},{5,1},{9,5},{13,9},{1,13},{6,2},{10,6},{... | collective-permute-start | bytes 196616 | tf_op jit(solution)/shard_map/ppermute | solution.py:21
  97.6 5.5 %collective-permute-start.26 = (bf16[6,1,256]{2,1,0:T(2,128)(2,1)S(1)}, bf16[6,1,256]{2,1,0:T(2,128)(2,1)S(1)}, u32[]{:S(2)}, u32[]{:S(2)}) collective-permute-start(bf16[6,1,256]{2,1,0:T(2,128)(2,1)S(1)} %get-tuple-element.93), channel_id=1, source_target_pairs={{0,1},{1,2},{2,3},{3,0},{4,5},{5,6},{6,7},{7,4},{8,9},{9,10},{10,1... | collective-permute-start | bytes 9224 | tf_op jit(solution)/shard_map/ppermute | solution.py:20
  98.6 4.5 %collective-permute-start.27 = (bf16[6,1,256]{2,1,0:T(2,128)(2,1)S(1)}, bf16[6,1,256]{2,1,0:T(2,128)(2,1)S(1)}, u32[]{:S(2)}, u32[]{:S(2)}) collective-permute-start(bf16[6,1,256]{2,1,0:T(2,128)(2,1)S(1)} %get-tuple-element.94), channel_id=1, source_target_pairs={{1,0},{2,1},{3,2},{0,3},{5,4},{6,5},{7,6},{4,7},{9,8},{10,9},{11,1... | collective-permute-start | bytes 9224 | tf_op jit(solution)/shard_map/ppermute | solution.py:21
  107.2 3.7 %collective-permute-start.28 = (bf16[1,256,128]{2,1,0:T(8,128)(2,1)S(1)}, bf16[1,256,128]{2,1,0:T(8,128)(2,1)S(1)}, u32[]{:S(2)}, u32[]{:S(2)}) collective-permute-start(bf16[1,256,128]{2,1,0:T(8,128)(2,1)S(1)} %get-tuple-element.49), channel_id=1, source_target_pairs={{0,4},{4,8},{8,12},{12,0},{1,5},{5,9},{9,13},{13,1},{2,6},{6,10},{... | collective-permute-start | bytes 196616 | tf_op jit(solution)/shard_map/ppermute | solution.py:20
  111.1 5.5 %collective-permute-start.30 = (bf16[10,1,128]{2,1,0:T(2,128)(2,1)S(1)}, bf16[10,1,128]{2,1,0:T(2,128)(2,1)S(1)}, u32[]{:S(2)}, u32[]{:S(2)}) collective-permute-start(bf16[10,1,128]{2,1,0:T(2,128)(2,1)S(1)} %get-tuple-element.41), channel_id=1, source_target_pairs={{0,1},{1,2},{2,3},{3,0},{4,5},{5,6},{6,7},{7,4},{8,9},{9,10},{10,1... | collective-permute-start | bytes 7688 | tf_op jit(solution)/shard_map/ppermute | solution.py:20
  112.0 4.5 %collective-permute-start.31 = (bf16[10,1,128]{2,1,0:T(2,128)(2,1)S(1)}, bf16[10,1,128]{2,1,0:T(2,128)(2,1)S(1)}, u32[]{:S(2)}, u32[]{:S(2)}) collective-permute-start(bf16[10,1,128]{2,1,0:T(2,128)(2,1)S(1)} %get-tuple-element.42), channel_id=1, source_target_pairs={{1,0},{2,1},{3,2},{0,3},{5,4},{6,5},{7,6},{4,7},{9,8},{10,9},{11,1... | collective-permute-start | bytes 7688 | tf_op jit(solution)/shard_map/ppermute | solution.py:21
  120.7 4.2 %collective-permute-start.32 = (bf16[12,8,256]{2,1,0:T(8,128)(2,1)S(1)}, bf16[12,8,256]{2,1,0:T(8,128)(2,1)S(1)}, u32[]{:S(2)}, u32[]{:S(2)}) collective-permute-start(bf16[12,8,256]{2,1,0:T(8,128)(2,1)S(1)} %fusion.92), channel_id=1, source_target_pairs={{0,16},{16,0},{1,17},{17,1},{2,18},{18,2},{3,19},{19,3},{4,20},{20... | collective-permute-start | bytes 147464 | tf_op jit(solution)/shard_map/ppermute | solution.py:29
  (12 other events, 37.7 us)
where the time goes:
time: 127 us; the launch traced here: 125 us
  starting transfers between devices  47.5 us (37%)
  waiting for transfers between devices  34.2 us (27%)
  matrix products  25 us (20%)
  local copies, waits for them, and re-layouts  10.1 us (8%)
  other arithmetic  7.71 us (6%)
    ppermute x16, waiting for transfers between devices, extended(): before = lax.ppermute(last, axis, up)  27.4 us
    ppermute x16, starting transfers between devices, extended(): after = lax.ppermute(first, axis, down)  26.9 us
    ppermute x16, starting transfers between devices, extended(): before = lax.ppermute(last, axis, up)  20.6 us
    dot_general x70, matrix products, convolve(): jnp.dot(window, kernel[offset], preferred_element_type=jnp.float32)  18.8 us
    unnamed x28, local copies, waits for them, and re-layouts  4.96 us
    slice x8, local copies, waits for them, and re-layouts, convolve(): padded[down:down + height, across:across + breadth]  4.5 us
    ppermute x1, waiting for transfers between devices, swapped(): return lax.ppermute(value, axis, pairs)  4.08 us
    dot_general x2, matrix products, network(): lax.dot_general(head, last_level.reshape(height * breadth, -1), (((0,), (...  3.02 us
  transfers between devices with their start and end apart: 33, of which 25 were waited for; matrix products, arithmetic and copies ran while one was open for 0% of the time, Pallas kernels for 0%

commit v1 on v0

v1 whole, which is shorter than its diff:
```python
import functools
import math

import jax
import jax.numpy as jnp
from jax import lax
from jax.experimental import pallas as pl
from jax.experimental.pallas import tpu as pltpu
from jax.sharding import PartitionSpec as P

sigma_data = 0.5
sigma_high = 2.0
sigma_low = 0.5

MESH = pl.DeviceIdType.MESH
bf16 = jnp.bfloat16
f32 = jnp.float32

HALO = 8
MESSAGES = ((0, 1), (0, -1), (1, 1), (1, -1), (-1, 1), (-1, -1), (1, 0), (-1, 0))


def precondition(sigma):
    total = sigma * sigma + sigma_data * sigma_data
    return (
        1.0 / math.sqrt(total),
        sigma_data * sigma_data / total,
        sigma * sigma_data / math.sqrt(total),
        math.log(sigma) / 4.0,
    )


def silu(x):
    half = 0.5 * x
    return half + half * jnp.tanh(half)


def dot(a, b):
    return jnp.dot(a, b, preferred_element_type=f32)


def dot_nt(a, b):
    return lax.dot_general(a, b, (((1,), (1,)), ((), ())), preferred_element_type=f32)


def kernel(
    n_lat,
    n_lon,
    start,
    prior,
    lift_w,
    gain,
    conv0a,
    expand,
    conv1a,
    conv1b,
    shrink,
    conv0b,
    head,
    out,
    w0a,
    w0b,
    w1a,
    w1b,
    wlift,
    whead,
    mine,
    edges1,
    lat1,
    rim1,
    state2,
    edges2,
    lat2,
    rim2,
    given_t,
    moved,
    shift,
    cells,
    lifted,
    first,
    widened,
    inner,
    merged,
    last,
    finished,
    arrived,
    wsem,
    ssem,
    rsem,
    swap_s,
    swap_r,
):
    section = lax.axis_index("section")
    lat = lax.axis_index("lat")
    lon = lax.axis_index("lon")
    diffuse = section == 1
    variables, rows, cols = start.shape[1:]
    c0 = lift_w.shape[-1]
    half = cols // 2
    wide = half + 2 * HALO
    pairs = rows // 2
    used = variables * rows
    lanes = given_t.shape[1]
    high = precondition(sigma_high)
    low = precondition(sigma_low)

    def target(dlat, dlon):
        return (section, lat + dlat, lax.rem(lon + dlon + n_lon, n_lon))

    def present(dlat):
        if dlat < 0:
            return lat > 0
        return lat < n_lat - 1

    def guarded(dlat, action):
        if dlat == 0:
            action()
        else:
            pl.when(present(dlat))(action)

    partner = (1 - section, lat, lon)

    barrier = pltpu.get_barrier_semaphore()
    pl.semaphore_signal(barrier, inc=1, device_id=partner, device_id_type=MESH)
    for dlat, dlon in MESSAGES:
        guarded(
            dlat,
            functools.partial(
                pl.semaphore_signal,
                barrier,
                inc=1,
                device_id=target(dlat, dlon),
                device_id_type=MESH,
            ),
        )

    copies = [
        pltpu.make_async_copy(
            conv0a.at[0], w0a.at[pl.ds(0, 3), :, :, pl.ds(0, c0)], wsem.at[0]
        ),
        pltpu.make_async_copy(
            conv0a.at[0], w0a.at[pl.ds(1, 3), :, :, pl.ds(c0, c0)], wsem.at[1]
        ),
        pltpu.make_async_copy(conv1a.at[0], w1a, wsem.at[2]),
        pltpu.make_async_copy(conv1b.at[0], w1b, wsem.at[3]),
        pltpu.make_async_copy(
            conv0b.at[0], w0b.at[pl.ds(0, 3), :, :, pl.ds(0, c0)], wsem.at[4]
        ),
        pltpu.make_async_copy(
            conv0b.at[0], w0b.at[pl.ds(1, 3), :, :, pl.ds(c0, c0)], wsem.at[5]
        ),
    ]
    for copy in copies:
        copy.start()
    for folded in (w0a, w0b):
        blank = jnp.zeros((3, c0, c0), bf16)
        folded[3, :, :, 0:c0] = blank
        folded[0, :, :, c0 : 2 * c0] = blank

    i = lax.broadcasted_iota(jnp.int32, (cols, cols), 0)
    j = lax.broadcasted_iota(jnp.int32, (cols, cols), 1)
    order = jnp.where(
        j == jnp.where(i < half, 2 * i, 2 * (i - half) + 1), 1.0, 0.0
    ).astype(bf16)

    def turned(x):
        flat = x.reshape(used, cols)
        if lanes > used:
            flat = jnp.concatenate([flat, jnp.zeros((lanes - used, cols), f32)], axis=0)
        return dot_nt(order, flat.astype(bf16))

    def straight(y):
        a = lax.broadcasted_iota(jnp.int32, (lanes, lanes), 0)
        b = lax.broadcasted_iota(jnp.int32, (lanes, lanes), 1)
        eye = jnp.where(a == b, 1.0, 0.0).astype(bf16)
        return dot(dot_nt(eye, y).astype(bf16), order)[:used]

    def borders(t, edges):
        edges[0] = jnp.concatenate([t[half - HALO : half], t[cols - HALO : cols]], axis=0).astype(bf16)
        edges[1] = jnp.concatenate([t[0:HALO], t[half : half + HALO]], axis=0).astype(bf16)

    given = start[0].astype(f32)
    scale = jnp.where(diffuse, high[0] * sigma_high, 1.0).astype(f32)
    state = turned(scale * given)
    prior_t = turned(prior[...].astype(f32))
    given_t[...] = turned(given)
    full = jnp.concatenate([state, prior_t], axis=1)
    mine[...] = full.astype(bf16)
    borders(full, edges1)

    pl.semaphore_wait(
        barrier,
        3 + jnp.where(lat > 0, 3, 0) + jnp.where(lat < n_lat - 1, 3, 0),
    )

    def message(step, index, block, edges, lat_in, rim_in):
        dlat, dlon = MESSAGES[index]
        if dlon == 0:
            source, landing = block, lat_in.at[0 if dlat > 0 else 1]
        else:
            side = 0 if dlon > 0 else 1
            source, landing = edges.at[side], rim_in.at[side, 1 - dlat]
        return pltpu.make_async_remote_copy(
            src_ref=source,
            dst_ref=landing,
            send_sem=ssem.at[step, index],
            recv_sem=rsem.at[step, index],
            device_id=target(dlat, dlon),
            device_id_type=MESH,
        )

    exchanges = (
        (0, mine, edges1, lat1, rim1),
        (1, state2, edges2, lat2, rim2),
    )

    def send(exchange):
        step, *refs = exchange
        for index, (dlat, _) in enumerate(MESSAGES):
            guarded(dlat, lambda index=index: message(step, index, *refs).start())

    def receive(exchange, indices):
        step, *refs = exchange
        for index in indices:
            dlat = MESSAGES[index][0]
            guarded(-dlat, lambda index=index: message(step, index, *refs).wait_recv())

    def settle(exchange):
        step, *refs = exchange
        for index, (dlat, _) in enumerate(MESSAGES):
            guarded(dlat, lambda index=index: message(step, index, *refs).wait_send())

    send(exchanges[0])

    spread_w = jnp.broadcast_to(
        lift_w[0].astype(f32)[:, None, :], (2 * variables, rows, c0)
    ).reshape(2 * used, c0)
    row_of = lax.rem(lax.broadcasted_iota(jnp.int32, (lanes, c0), 0), rows)
    for part in range(2):
        piece = spread_w[part * used : (part + 1) * used]
        if lanes > used:
            piece = jnp.concatenate([piece, jnp.zeros((lanes - used, c0), f32)], axis=0)
        for r in range(rows):
            wlift[
                r // 2, part * lanes : (part + 1) * lanes, (r % 2) * c0 : (r % 2 + 1) * c0
            ] = jnp.where(row_of == r, piece, 0.0).astype(bf16)
    v_id = lax.broadcasted_iota(jnp.int32, (variables, lanes), 0)
    l_id = lax.broadcasted_iota(jnp.int32, (variables, lanes), 1)
    spreading = jnp.where((l_id >= v_id * rows) & (l_id < (v_id + 1) * rows), 1.0, 0.0).astype(bf16)
    spread_h = dot(head[0], spreading)
    lane_row = lax.rem(lax.broadcasted_iota(jnp.int32, (c0, lanes), 1), rows)
    for r in range(rows):
        whead[r * c0 : (r + 1) * c0, :] = jnp.where(lane_row == r, spread_h, 0.0).astype(bf16)
    expand_w = expand[0]
    shrink_w = jnp.concatenate([shrink[0], shrink[0]], axis=1)

    def inside(index):
        return jnp.logical_not(
            ((index < 0) & (lat == 0)) | ((index >= pairs) & (lat == n_lat - 1))
        )

    def masked(index, value):
        return jnp.where(inside(index), value, 0.0)

    def keep_fine(buffer, index, even, odd):
        buffer[0, index] = pltpu.roll(odd, 1, 0).astype(bf16)
        buffer[1, index] = even.astype(bf16)
        buffer[2, index] = odd.astype(bf16)
        buffer[3, index] = pltpu.roll(even, wide - 1, 0).astype(bf16)

    def keep_coarse(buffer, index, value):
        buffer[0, index] = pltpu.roll(value, 1, 0).astype(bf16)
        buffer[1, index] = value.astype(bf16)
        buffer[2, index] = pltpu.roll(value, wide - 1, 0).astype(bf16)

    def fine_window(buffer, index):
        def row(variant, q):
            at = index + (0, 1, 1, 2)[q]
            lane = (c0, 0, c0, 0)[q]
            return buffer[variant, at, :, lane : lane + c0]

        return jnp.concatenate(
            [
                jnp.concatenate([row(v + b, q) for q in range(4) for b in range(3)], axis=1)
                for v in range(2)
            ],
            axis=0,
        )

    def coarse_window(buffer, index):
        return jnp.concatenate(
            [buffer[b, index + a] for a in range(3) for b in range(3)], axis=1
        )

    def network(state_of, exchange):
        def assemble(slot):
            middle, left, right = state_of(slot)
            middle, left, right = (x.astype(f32) for x in (middle, left, right))
            cells[slot] = jnp.concatenate(
                [
                    left[:HALO],
                    middle[:half],
                    right[:HALO],
                    left[HALO:],
                    middle[half:],
                    right[HALO:],
                ],
                axis=0,
            ).astype(bf16)

        def lift_slot(slot):
            assemble(slot)

            def lift(p, carry):
                value = silu(dot(cells[slot], wlift[p]) + shift[...])
                if slot != 1:
                    value = masked((slot - 1) * pairs + p, value)
                keep_fine(lifted, slot * pairs + p, value[:wide], value[wide:])
                return carry

            lax.fori_loop(0, pairs, lift, 0)

        receive(exchange, (0, 1))
        lift_slot(1)
        receive(exchange, range(2, len(MESSAGES)))
        lift_slot(0)
        lift_slot(2)

        def down(step, carry):
            n = 2
            acc = dot(
                jnp.concatenate([fine_window(lifted, step * n + k) for k in range(n)], axis=0),
                w0a[...].reshape(12 * c0, 2 * c0),
            )
            value = silu(acc).astype(bf16)
            for k in range(n):
                index = step * n + k
                even = value[2 * k * wide : (2 * k + 1) * wide]
                odd = value[(2 * k + 1) * wide : (2 * k + 2) * wide]
                first[index, 0] = even
                first[index, 1] = odd
                total = even.astype(f32) + odd.astype(f32)
                pooled = ((total[:, :c0] + total[:, c0:]) * 0.25).astype(bf16)
                keep_coarse(widened, index, masked(index - (pairs - 1), dot(pooled, expand_w)))
            return carry

        if exchange[0] == 0:
            copies[0].wait()
            copies[1].wait()
        lax.fori_loop(0, (3 * pairs - 2) // 2, down, 0)

        def coarse_a(step, carry):
            n = 4
            acc = dot(
                jnp.concatenate([coarse_window(widened, step * n + k) for k in range(n)], axis=0),
                w1a[...].reshape(9 * w1a.shape[1], w1a.shape[2]),
            )
            value = silu(acc)
            for k in range(n):
                index = step * n + k
                keep_coarse(
                    inner, index, masked(index - (pairs - 2), value[k * wide : (k + 1) * wide])
                )
            return carry

        if exchange[0] == 0:
            copies[2].wait()
        lax.fori_loop(0, (3 * pairs - 4) // 4, coarse_a, 0)

        def coarse_b(step, carry):
            n = 3
            acc = dot(
                jnp.concatenate([coarse_window(inner, step * n + k) for k in range(n)], axis=0),
                w1b[...].reshape(9 * w1b.shape[1], w1b.shape[2]),
            )
            skip = jnp.concatenate([widened[1, step * n + k + 2] for k in range(n)], axis=0)
            projected = dot((silu(acc) + skip.astype(f32)).astype(bf16), shrink_w)
            for k in range(n):
                index = step * n + k
                piece = projected[k * wide : (k + 1) * wide]
                even = masked(index - 1, piece + first[index + 2, 0].astype(f32))
                odd = masked(index - 1, piece + first[index + 2, 1].astype(f32))
                keep_fine(merged, index, even, odd)
            return carry

        if exchange[0] == 0:
            copies[3].wait()
        lax.fori_loop(0, (pairs + 2) // 3, coarse_b, 0)

        def up(step, carry):
            n = 2
            acc = dot(
                jnp.concatenate([fine_window(merged, step * n + k) for k in range(n)], axis=0),
                w0b[...].reshape(12 * c0, 2 * c0),
            )
            value = silu(acc).astype(bf16)
            for k in range(n):
                last[step * n + k] = value[2 * k * wide : (2 * k + 2) * wide]
            return carry

        if exchange[0] == 0:
            copies[4].wait()
            copies[5].wait()
        lax.fori_loop(0, pairs // 2, up, 0)
        result = dot(jnp.concatenate([last[p] for p in range(pairs)], axis=1), whead[...])
        return jnp.concatenate(
            [result[HALO : HALO + half], result[wide + HALO : wide + HALO + half]], axis=0
        )

    def first_state(slot):
        middle = mine[...] if slot == 1 else lat1[0 if slot == 0 else 1]
        return middle, rim1[0, slot], rim1[1, slot]

    def second_state(slot):
        other = first_state(slot)
        middle = state2[...] if slot == 1 else lat2[0 if slot == 0 else 1]
        new = (middle, rim2[0, slot], rim2[1, slot])
        return tuple(
            jnp.concatenate([a, b[:, lanes:]], axis=1) for a, b in zip(new, other)
        )

    gains = jnp.concatenate([gain[...], gain[...]], axis=1)
    shift[...] = jnp.where(diffuse, high[3], 0.0).astype(f32) * gains
    first_out = network(first_state, exchanges[0])
    settle(exchanges[0])

    swap = pltpu.make_async_remote_copy(
        src_ref=finished,
        dst_ref=arrived,
        send_sem=swap_s,
        recv_sem=swap_r,
        device_id=partner,
        device_id_type=MESH,
    )

    @pl.when(jnp.logical_not(diffuse))
    def _():
        finished[...] = straight(first_out.astype(bf16)).astype(bf16)
        swap.start()

    @pl.when(diffuse)
    def _():
        noisy = sigma_high * given_t[...]
        first_denoised = high[1] * noisy + high[2] * first_out
        fresh = noisy + (sigma_low - sigma_high) / sigma_high * (noisy - first_denoised)
        moved[...] = fresh
        second_input = low[0] * fresh
        state2[...] = second_input.astype(bf16)
        borders(second_input, edges2)
        send(exchanges[1])
        shift[...] = low[3] * gains
        second_out = network(second_state, exchanges[1])
        second_denoised = low[1] * moved[...] + low[2] * second_out
        sample = mine[:, lanes:].astype(f32) + second_denoised
        finished[...] = straight(sample.astype(bf16)).astype(bf16)
        swap.start()
        settle(exchanges[1])

    swap.wait()
    out[0] = arrived[...].astype(f32).reshape(variables, rows, cols).astype(bf16)


def on_device(
    n_lat,
    n_lon,
    start,
    prior_mean,
    lift_w,
    noise_gain,
    conv0a,
    expand,
    conv1a,
    conv1b,
    shrink,
    conv0b,
    head,
):
    variables, rows, cols = prior_mean.shape
    c0, c1 = expand.shape[1:]
    pairs = rows // 2
    half = cols // 2
    wide = half + 2 * HALO
    lanes = -(-variables * rows // 128) * 128
    used = variables * rows
    assert pairs == 4 and 2 * c0 == c1
    split = (1, 3, 3, c0, c0)
    vmem = pl.BlockSpec(memory_space=pltpu.VMEM)
    hbm = pl.BlockSpec(memory_space=pl.ANY)
    scratch = [
        pltpu.VMEM((4, 3, c0, 2 * c0), bf16),
        pltpu.VMEM((4, 3, c0, 2 * c0), bf16),
        pltpu.VMEM((9, c1, c1), bf16),
        pltpu.VMEM((9, c1, c1), bf16),
        pltpu.VMEM((pairs, 2 * lanes, 2 * c0), bf16),
        pltpu.VMEM((rows * c0, lanes), bf16),
        pltpu.VMEM((cols, 2 * lanes), bf16),
        pltpu.VMEM((2, 2 * HALO, 2 * lanes), bf16),
        pltpu.VMEM((2, cols, 2 * lanes), bf16),
        pltpu.VMEM((2, 3, 2 * HALO, 2 * lanes), bf16),
        pltpu.VMEM((cols, lanes), bf16),
        pltpu.VMEM((2, 2 * HALO, lanes), bf16),
        pltpu.VMEM((2, cols, lanes), bf16),
        pltpu.VMEM((2, 3, 2 * HALO, lanes), bf16),
        pltpu.VMEM((cols, lanes), f32),
        pltpu.VMEM((cols, lanes), f32),
        pltpu.VMEM((1, 2 * c0), f32),
        pltpu.VMEM((3, 2 * wide, 2 * lanes), bf16),
        pltpu.VMEM((4, 3 * pairs, wide, 2 * c0), bf16),
        pltpu.VMEM((3 * pairs - 2, 2, wide, 2 * c0), bf16),
        pltpu.VMEM((3, 3 * pairs - 2, wide, c1), bf16),
        pltpu.VMEM((3, 3 * pairs - 4, wide, c1), bf16),
        pltpu.VMEM((4, pairs + 2, wide, 2 * c0), bf16),
        pltpu.VMEM((pairs, 2 * wide, 2 * c0), bf16),
        pltpu.VMEM((used, cols), bf16),
        pltpu.VMEM((used, cols), bf16),
        pltpu.SemaphoreType.DMA((6,)),
        pltpu.SemaphoreType.DMA((2, len(MESSAGES))),
        pltpu.SemaphoreType.DMA((2, len(MESSAGES))),
        pltpu.SemaphoreType.DMA,
        pltpu.SemaphoreType.DMA,
    ]
    return pl.pallas_call(
        functools.partial(kernel, n_lat, n_lon),
        out_shape=jax.ShapeDtypeStruct((1, variables, rows, cols), bf16),
        in_specs=[vmem, vmem, vmem, vmem, hbm, vmem, hbm, hbm, vmem, hbm, vmem],
        out_specs=vmem,
        scratch_shapes=scratch,
        compiler_params=pltpu.CompilerParams(
            collective_id=0, has_side_effects=True, vmem_limit_bytes=48 * 2**20
        ),
    )(
        start,
        prior_mean,
        lift_w,
        noise_gain,
        conv0a.reshape(split),
        expand,
        conv1a,
        conv1b,
        shrink,
        conv0b.reshape(split),
        head,
    )


def solution(mesh):
    placed = (
        P("section", None, "lat", "lon"),
        P(None, "lat", "lon"),
        P("section", None, None),
        P("section", None),
        P("section", None, None, None),
        P("section", None, None),
        P("section", None, None, None),
        P("section", None, None, None),
        P("section", None, None),
        P("section", None, None, None),
        P("section", None, None),
    )
    return jax.shard_map(
        functools.partial(on_device, mesh.shape["lat"], mesh.shape["lon"]),
        mesh=mesh,
        in_specs=placed,
        out_specs=P("section", None, "lat", "lon"),
        check_vma=False,
    )
```

time: 127 us -> 52.9 us (0.42)
  starting transfers between devices: 47.5 us -> 0 us
  Pallas kernels: 0 us -> 41.9 us
  waiting for transfers between devices: 34.2 us -> 0 us
  matrix products: 25 us -> 0 us
  other arithmetic: 7.71 us -> 0 us
    ppermute x33 -> x0, starting transfers between devices: 47.5 us -> none  [the longest x16 26.9 us: extended(): after = lax.ppermute(first, axis, down)]
    pallas_call x0 -> x1, Pallas kernels: none -> 41.9 us  [on_device(): pl.pallas_call(functools.partial(kernel, n_lat, n_lon), out_shape=jax.Sha...]
    ppermute x33 -> x0, waiting for transfers between devices: 34.2 us -> none  [the longest x16 27.4 us: extended(): before = lax.ppermute(last, axis, up)]
    dot_general x78 -> x0, matrix products: 25 us -> none  [the longest x70 18.8 us: convolve(): jnp.dot(window, kernel[offset], preferred_element_type=jnp.float32)]
    unnamed x28 -> x22, local copies, waits for them, and re-layouts: 4.96 us -> 10.5 us
    slice x16 -> x0, local copies, waits for them, and re-layouts: 4.59 us -> none  [the longest x8 4.5 us: convolve(): padded[down:down + height, across:across + breadth]]
    convert_element_type x8 -> x0, other arithmetic: 2.6 us -> none  [the longest x1 0.84 us: on_device(): state = jnp.where(diffuse, high[0] * noisy, given).astype(jnp.bfloat16)]
    select_n x9 -> x0, other arithmetic: 2.06 us -> none  [the longest x8 2.01 us: band_edges(): return jnp.where(outside.reshape(layout), jnp.zeros((), field.dtype), field)]
  transfers between devices with their start and end apart: 33 -> 0, of which waited for: 25 -> 0; matrix products, arithmetic and copies ran while one was open for 0% -> 0% of each run, Pallas kernels for 0% -> 0%
where the time goes in v1:
time: 52.9 us; the launch traced here: 52.4 us
  Pallas kernels  41.9 us (79%)
  local copies, waits for them, and re-layouts  10.5 us (20%)
    pallas_call x1, Pallas kernels, on_device(): pl.pallas_call(functools.partial(kernel, n_lat, n_lon), out_shape=jax.Sha...  41.9 us
    unnamed x22, local copies, waits for them, and re-layouts  10.5 us

profile of v1, /device:TPU:0, one launch (start us, length us, event | category | flops | bytes accessed | tf_op | source)
XLA Modules:
  0.0 52.4 jit_solution(2341928577453969826)
XLA Ops:
  0.0 0.8 %copy.12.head = bf16[1,128,12]{2,1,0:T(8,128)(2,1)S(1)} copy(bf16[1,128,12]{1,2,0:T(8,128)(2,1)} %param.21) | data formatting | bytes 6144 | tf_op args[10]
  0.8 0.0 copy-start
  0.8 1.3 %copy-done = bf16[1,9,256,256]{3,2,1,0:T(8,128)(2,1)S(1)} copy-done((bf16[1,9,256,256]{3,2,1,0:T(8,128)(2,1)S(1)}, bf16[1,9,256,256]{3,2,1,0:T(8,128)(2,1)}, u32[]{:S(2)}) %copy-start) | copy-done | bytes 1179672
  2.1 0.0 copy-start.1
  2.1 1.3 %copy-done.1 = bf16[1,9,256,256]{3,2,1,0:T(8,128)(2,1)S(1)} copy-done((bf16[1,9,256,256]{3,2,1,0:T(8,128)(2,1)S(1)}, bf16[1,9,256,256]{3,2,1,0:T(8,128)(2,1)}, u32[]{:S(2)}) %copy-start.1) | copy-done | bytes 1179672
  3.4 0.0 copy-start.2
  3.4 1.0 %copy-done.2 = bf16[1,9,128,128]{3,2,1,0:T(8,128)(2,1)S(1)} copy-done((bf16[1,9,128,128]{3,2,1,0:T(8,128)(2,1)S(1)}, bf16[1,9,128,128]{3,2,1,0:T(8,128)(2,1)}, u32[]{:S(2)}) %copy-start.2) | copy-done | bytes 294936
  4.3 0.0 copy-start.3
  4.3 1.0 %copy-done.3 = bf16[1,9,128,128]{3,2,1,0:T(8,128)(2,1)S(1)} copy-done((bf16[1,9,128,128]{3,2,1,0:T(8,128)(2,1)S(1)}, bf16[1,9,128,128]{3,2,1,0:T(8,128)(2,1)}, u32[]{:S(2)}) %copy-start.3) | copy-done | bytes 294936
  5.3 0.0 copy-start.4
  5.3 0.8 %copy-done.4 = bf16[1,128,256]{2,1,0:T(8,128)(2,1)S(1)} copy-done((bf16[1,128,256]{2,1,0:T(8,128)(2,1)S(1)}, bf16[1,128,256]{2,1,0:T(8,128)(2,1)}, u32[]{:S(2)}) %copy-start.4) | copy-done | bytes 65560
  6.1 0.0 copy-start.5
  6.1 0.8 %copy-done.5 = bf16[1,256,128]{2,1,0:T(8,128)(2,1)S(1)} copy-done((bf16[1,256,128]{2,1,0:T(8,128)(2,1)S(1)}, bf16[1,256,128]{2,1,0:T(8,128)(2,1)}, u32[]{:S(2)}) %copy-start.5) | copy-done | bytes 65560
  7.0 0.0 copy-start.6
  7.0 0.8 %copy-done.6 = bf16[1,12,8,256]{3,2,1,0:T(8,128)(2,1)S(1)} copy-done((bf16[1,12,8,256]{3,2,1,0:T(8,128)(2,1)S(1)}, bf16[1,12,8,256]{3,2,1,0:T(8,128)(2,1)}, u32[]{:S(2)}) %copy-start.6) | copy-done | bytes 49176
  7.8 0.0 copy-start.7
  7.8 0.8 %copy-done.7 = bf16[12,8,256]{2,1,0:T(8,128)(2,1)S(1)} copy-done((bf16[12,8,256]{2,1,0:T(8,128)(2,1)S(1)}, bf16[12,8,256]{2,1,0:T(8,128)(2,1)}, u32[]{:S(2)}) %copy-start.7) | copy-done | bytes 49176
  8.6 0.0 copy-start.8
  8.6 0.7 %copy-done.8 = bf16[1,24,128]{2,1,0:T(8,128)(2,1)S(1)} copy-done((bf16[1,24,128]{2,1,0:T(8,128)(2,1)S(1)}, bf16[1,24,128]{2,1,0:T(8,128)(2,1)}, u32[]{:S(2)}) %copy-start.8) | copy-done | bytes 6168
  9.3 0.0 copy-start.9
  9.3 0.7 %copy-done.9 = f32[1,128]{1,0:T(1,128)S(1)} copy-done((f32[1,128]{1,0:T(1,128)S(1)}, f32[1,128]{1,0:T(1,128)}, u32[]{:S(2)}) %copy-start.9) | copy-done | bytes 536
  9.9 41.9 %shard_map.109 = bf16[1,12,8,256]{3,2,1,0:T(8,128)(2,1)S(1)} custom-call(bf16[1,12,8,256]{3,2,1,0:T(8,128)(2,1)S(1)} %copy-done.6, bf16[12,8,256]{2,1,0:T(8,128)(2,1)S(1)} %copy-done.7, bf16[1,24,128]{2,1,0:T(8,128)(2,1)S(1)} %copy-done.8, f32[1,128]{1,0:T(1,128)S(1)} %copy-done.9, bf16[1,3,3,128,128]{4,3,2,1,0:T(8,128)(2,1)S(1)} %bitcast.2, ...), custom_call_target="tpu_custom_call" | custom-call | tf_op jit(solution)/shard_map/pallas_call | solution.py:522
  51.8 0.6 %copy.14 = bf16[1,12,8,256]{3,2,1,0:T(8,128)(2,1)} copy(bf16[1,12,8,256]{3,2,1,0:T(8,128)(2,1)S(1)} %shard_map.109) | data formatting | bytes 98304
Async XLA Ops:
  0.8 1.3 %copy-start = (bf16[1,9,256,256]{3,2,1,0:T(8,128)(2,1)S(1)}, bf16[1,9,256,256]{3,2,1,0:T(8,128)(2,1)}, u32[]{:S(2)}) copy-start(bf16[1,9,256,256]{3,2,1,0:T(8,128)(2,1)} %conv1a.1) | copy-start | bytes 3538948
  2.1 1.3 %copy-start.1 = (bf16[1,9,256,256]{3,2,1,0:T(8,128)(2,1)S(1)}, bf16[1,9,256,256]{3,2,1,0:T(8,128)(2,1)}, u32[]{:S(2)}) copy-start(bf16[1,9,256,256]{3,2,1,0:T(8,128)(2,1)} %conv1b.1) | copy-start | bytes 3538948
  3.4 1.0 %copy-start.2 = (bf16[1,9,128,128]{3,2,1,0:T(8,128)(2,1)S(1)}, bf16[1,9,128,128]{3,2,1,0:T(8,128)(2,1)}, u32[]{:S(2)}) copy-start(bf16[1,9,128,128]{3,2,1,0:T(8,128)(2,1)} %param.15) | copy-start | bytes 884740
  4.3 1.0 %copy-start.3 = (bf16[1,9,128,128]{3,2,1,0:T(8,128)(2,1)S(1)}, bf16[1,9,128,128]{3,2,1,0:T(8,128)(2,1)}, u32[]{:S(2)}) copy-start(bf16[1,9,128,128]{3,2,1,0:T(8,128)(2,1)} %param.20) | copy-start | bytes 884740
  5.3 0.8 %copy-start.4 = (bf16[1,128,256]{2,1,0:T(8,128)(2,1)S(1)}, bf16[1,128,256]{2,1,0:T(8,128)(2,1)}, u32[]{:S(2)}) copy-start(bf16[1,128,256]{2,1,0:T(8,128)(2,1)} %expand.1) | copy-start | bytes 196612
  6.1 0.8 %copy-start.5 = (bf16[1,256,128]{2,1,0:T(8,128)(2,1)S(1)}, bf16[1,256,128]{2,1,0:T(8,128)(2,1)}, u32[]{:S(2)}) copy-start(bf16[1,256,128]{2,1,0:T(8,128)(2,1)} %shrink.1) | copy-start | bytes 196612
  7.0 0.8 %copy-start.6 = (bf16[1,12,8,256]{3,2,1,0:T(8,128)(2,1)S(1)}, bf16[1,12,8,256]{3,2,1,0:T(8,128)(2,1)}, u32[]{:S(2)}) copy-start(bf16[1,12,8,256]{3,2,1,0:T(8,128)(2,1)} %start.1) | copy-start | bytes 147460
  7.8 0.8 %copy-start.7 = (bf16[12,8,256]{2,1,0:T(8,128)(2,1)S(1)}, bf16[12,8,256]{2,1,0:T(8,128)(2,1)}, u32[]{:S(2)}) copy-start(bf16[12,8,256]{2,1,0:T(8,128)(2,1)} %prior.1) | copy-start | bytes 147460
  8.6 0.7 %copy-start.8 = (bf16[1,24,128]{2,1,0:T(8,128)(2,1)S(1)}, bf16[1,24,128]{2,1,0:T(8,128)(2,1)}, u32[]{:S(2)}) copy-start(bf16[1,24,128]{2,1,0:T(8,128)(2,1)} %lift_w.1) | copy-start | bytes 18436
  9.3 0.7 %copy-start.9 = (f32[1,128]{1,0:T(1,128)S(1)}, f32[1,128]{1,0:T(1,128)}, u32[]{:S(2)}) copy-start(f32[1,128]{1,0:T(1,128)} %gain.1) | copy-start | bytes 1540

commit v2 on v1

--- a/solution.py
+++ b/solution.py
@@ -46,18 +46,25 @@
 def kernel(
     n_lat,
     n_lon,
+    start_hbm,
+    prior_hbm,
+    lift_w_hbm,
+    gain_hbm,
+    conv0a,
+    expand_hbm,
+    conv1a,
+    conv1b,
+    shrink_hbm,
+    conv0b,
+    head_hbm,
+    out,
     start,
     prior,
     lift_w,
     gain,
-    conv0a,
     expand,
-    conv1a,
-    conv1b,
     shrink,
-    conv0b,
     head,
-    out,
     w0a,
     w0b,
     w1a,
@@ -84,6 +91,7 @@
     last,
     finished,
     arrived,
+    osem,
     wsem,
     ssem,
     rsem,
@@ -94,7 +102,7 @@
     lat = lax.axis_index("lat")
     lon = lax.axis_index("lon")
     diffuse = section == 1
-    variables, rows, cols = start.shape[1:]
+    variables, rows, cols = prior.shape
     c0 = lift_w.shape[-1]
     half = cols // 2
     wide = half + 2 * HALO
@@ -119,6 +127,23 @@
             pl.when(present(dlat))(action)
 
     partner = (1 - section, lat, lon)
+
+    small = [
+        pltpu.make_async_copy(source, landing, osem.at[k])
+        for k, (source, landing) in enumerate(
+            (
+                (start_hbm.at[0], start),
+                (prior_hbm, prior),
+                (lift_w_hbm.at[0], lift_w),
+                (gain_hbm, gain),
+                (head_hbm.at[0], head),
+                (expand_hbm.at[0], expand),
+                (shrink_hbm.at[0], shrink),
+            )
+        )
+    ]
+    for copy in small:
+        copy.start()
 
     barrier = pltpu.get_barrier_semaphore()
     pl.semaphore_signal(barrier, inc=1, device_id=partner, device_id_type=MESH)
@@ -179,7 +204,9 @@
         edges[0] = jnp.concatenate([t[half - HALO : half], t[cols - HALO : cols]], axis=0).astype(bf16)
         edges[1] = jnp.concatenate([t[0:HALO], t[half : half + HALO]], axis=0).astype(bf16)
 
-    given = start[0].astype(f32)
+    small[0].wait()
+    small[1].wait()
+    given = start[...].astype(f32)
     scale = jnp.where(diffuse, high[0] * sigma_high, 1.0).astype(f32)
     state = turned(scale * given)
     prior_t = turned(prior[...].astype(f32))
@@ -232,8 +259,10 @@
 
     send(exchanges[0])
 
+    for copy in small[2:]:
+        copy.wait()
     spread_w = jnp.broadcast_to(
-        lift_w[0].astype(f32)[:, None, :], (2 * variables, rows, c0)
+        lift_w[...].astype(f32)[:, None, :], (2 * variables, rows, c0)
     ).reshape(2 * used, c0)
     row_of = lax.rem(lax.broadcasted_iota(jnp.int32, (lanes, c0), 0), rows)
     for part in range(2):
@@ -247,12 +276,14 @@
     v_id = lax.broadcasted_iota(jnp.int32, (variables, lanes), 0)
     l_id = lax.broadcasted_iota(jnp.int32, (variables, lanes), 1)
     spreading = jnp.where((l_id >= v_id * rows) & (l_id < (v_id + 1) * rows), 1.0, 0.0).astype(bf16)
-    spread_h = dot(head[0], spreading)
+    spread_h = lax.dot_general(
+        head[...], spreading, (((0,), (0,)), ((), ())), preferred_element_type=f32
+    )
     lane_row = lax.rem(lax.broadcasted_iota(jnp.int32, (c0, lanes), 1), rows)
     for r in range(rows):
         whead[r * c0 : (r + 1) * c0, :] = jnp.where(lane_row == r, spread_h, 0.0).astype(bf16)
-    expand_w = expand[0]
-    shrink_w = jnp.concatenate([shrink[0], shrink[0]], axis=1)
+    expand_w = expand[...]
+    shrink_w = jnp.concatenate([shrink[...], shrink[...]], axis=1)
 
     def inside(index):
         return jnp.logical_not(
@@ -260,6 +291,8 @@
         )
 
     def masked(index, value):
+        if 0 <= index < pairs:
+            return value
         return jnp.where(inside(index), value, 0.0)
 
     def keep_fine(buffer, index, even, odd):
@@ -311,22 +344,18 @@
         def lift_slot(slot):
             assemble(slot)
 
-            def lift(p, carry):
+            def lift(p):
                 value = silu(dot(cells[slot], wlift[p]) + shift[...])
-                if slot != 1:
-                    value = masked((slot - 1) * pairs + p, value)
+                value = masked((slot - 1) * pairs + p, value)
                 keep_fine(lifted, slot * pairs + p, value[:wide], value[wide:])
-                return carry
-
-            lax.fori_loop(0, pairs, lift, 0)
+
+            for p in range(pairs):
+                lift(p)
 
         receive(exchange, (0, 1))
         lift_slot(1)
-        receive(exchange, range(2, len(MESSAGES)))
-        lift_slot(0)
-        lift_slot(2)
-
-        def down(step, carry):
+
+        def down(step):
             n = 2
             acc = dot(
                 jnp.concatenate([fine_window(lifted, step * n + k) for k in range(n)], axis=0),
@@ -342,14 +371,19 @@
                 total = even.astype(f32) + odd.astype(f32)
                 pooled = ((total[:, :c0] + total[:, c0:]) * 0.25).astype(bf16)
                 keep_coarse(widened, index, masked(index - (pairs - 1), dot(pooled, expand_w)))
-            return carry
 
         if exchange[0] == 0:
             copies[0].wait()
             copies[1].wait()
-        lax.fori_loop(0, (3 * pairs - 2) // 2, down, 0)
-
-        def coarse_a(step, carry):
+        down(pairs // 2)
+        receive(exchange, range(2, len(MESSAGES)))
+        lift_slot(0)
+        lift_slot(2)
+        for step in range((3 * pairs - 2) // 2):
+            if step != pairs // 2:
+                down(step)
+
+        def coarse_a(step):
             n = 4
             acc = dot(
                 jnp.concatenate([coarse_window(widened, step * n + k) for k in range(n)], axis=0),
@@ -361,13 +395,13 @@
                 keep_coarse(
                     inner, index, masked(index - (pairs - 2), value[k * wide : (k + 1) * wide])
                 )
-            return carry
 
         if exchange[0] == 0:
             copies[2].wait()
-        lax.fori_loop(0, (3 * pairs - 4) // 4, coarse_a, 0)
-
-        def coarse_b(step, carry):
+        for step in range((3 * pairs - 4) // 4):
+            coarse_a(step)
+
+        def coarse_b(step):
             n = 3
             acc = dot(
                 jnp.concatenate([coarse_window(inner, step * n + k) for k in range(n)], axis=0),
@@ -381,13 +415,13 @@
                 even = masked(index - 1, piece + first[index + 2, 0].astype(f32))
                 odd = masked(index - 1, piece + first[index + 2, 1].astype(f32))
                 keep_fine(merged, index, even, odd)
-            return carry
 
         if exchange[0] == 0:
             copies[3].wait()
-        lax.fori_loop(0, (pairs + 2) // 3, coarse_b, 0)
-
-        def up(step, carry):
+        for step in range((pairs + 2) // 3):
+            coarse_b(step)
+
+        def up(step):
             n = 2
             acc = dot(
                 jnp.concatenate([fine_window(merged, step * n + k) for k in range(n)], axis=0),
@@ -396,12 +430,12 @@
             value = silu(acc).astype(bf16)
             for k in range(n):
                 last[step * n + k] = value[2 * k * wide : (2 * k + 2) * wide]
-            return carry
 
         if exchange[0] == 0:
             copies[4].wait()
             copies[5].wait()
-        lax.fori_loop(0, pairs // 2, up, 0)
+        for step in range(pairs // 2):
+            up(step)
         result = dot(jnp.concatenate([last[p] for p in range(pairs)], axis=1), whead[...])
         return jnp.concatenate(
             [result[HALO : HALO + half], result[wide + HALO : wide + HALO + half]], axis=0
@@ -485,8 +519,16 @@
     assert pairs == 4 and 2 * c0 == c1
     split = (1, 3, 3, c0, c0)
     vmem = pl.BlockSpec(memory_space=pltpu.VMEM)
+    head_t = jnp.swapaxes(head, 1, 2)
     hbm = pl.BlockSpec(memory_space=pl.ANY)
     scratch = [
+        pltpu.VMEM(start.shape[1:], bf16),
+        pltpu.VMEM(prior_mean.shape, bf16),
+        pltpu.VMEM(lift_w.shape[1:], bf16),
+        pltpu.VMEM(noise_gain.shape, f32),
+        pltpu.VMEM(expand.shape[1:], bf16),
+        pltpu.VMEM(shrink.shape[1:], bf16),
+        pltpu.VMEM(head_t.shape[1:], bf16),
         pltpu.VMEM((4, 3, c0, 2 * c0), bf16),
         pltpu.VMEM((4, 3, c0, 2 * c0), bf16),
         pltpu.VMEM((9, c1, c1), bf16),
@@ -513,6 +555,7 @@
         pltpu.VMEM((pairs, 2 * wide, 2 * c0), bf16),
         pltpu.VMEM((used, cols), bf16),
         pltpu.VMEM((used, cols), bf16),
+        pltpu.SemaphoreType.DMA((7,)),
         pltpu.SemaphoreType.DMA((6,)),
         pltpu.SemaphoreType.DMA((2, len(MESSAGES))),
         pltpu.SemaphoreType.DMA((2, len(MESSAGES))),
@@ -522,11 +565,11 @@
     return pl.pallas_call(
         functools.partial(kernel, n_lat, n_lon),
         out_shape=jax.ShapeDtypeStruct((1, variables, rows, cols), bf16),
-        in_specs=[vmem, vmem, vmem, vmem, hbm, vmem, hbm, hbm, vmem, hbm, vmem],
+        in_specs=[hbm] * 11,
         out_specs=vmem,
         scratch_shapes=scratch,
         compiler_params=pltpu.CompilerParams(
-            collective_id=0, has_side_effects=True, vmem_limit_bytes=48 * 2**20
+            collective_id=0, has_side_effects=True, vmem_limit_bytes=60 * 2**20
         ),
     )(
         start,
@@ -539,7 +582,7 @@
         conv1b,
         shrink,
         conv0b.reshape(split),
-        head,
+        head_t,
     )
 
 

time: 52.9 us -> 43.4 us (0.82)
  local copies, waits for them, and re-layouts: 10.5 us -> 1.42 us
    unnamed x22 -> x1, local copies, waits for them, and re-layouts: 10.5 us -> 1.42 us
where the time goes in v2:
time: 43.4 us; the launch traced here: 43.2 us
  Pallas kernels  41.8 us (96%)
  local copies, waits for them, and re-layouts  1.42 us (3%)
    pallas_call x1, Pallas kernels, on_device(): pl.pallas_call(functools.partial(kernel, n_lat, n_lon), out_shape=jax.Sha...  41.8 us
    unnamed x1, local copies, waits for them, and re-layouts  1.42 us

profile of v2, /device:TPU:0, one launch (start us, length us, event | category | flops | bytes accessed | tf_op | source)
XLA Modules:
  0.0 43.2 jit_solution(5312971111739961718)
XLA Ops:
  0.0 41.8 %shard_map.109 = bf16[1,12,8,256]{3,2,1,0:T(8,128)(2,1)} custom-call(bf16[1,12,8,256]{3,2,1,0:T(8,128)(2,1)} %start_hbm.1, bf16[12,8,256]{2,1,0:T(8,128)(2,1)} %prior_hbm.1, bf16[1,24,128]{2,1,0:T(8,128)(2,1)} %lift_w_hbm.1, f32[1,128]{1,0:T(1,128)} %gain_hbm.1, bf16[1,3,3,128,128]{4,3,2,1,0:T(8,128)(2,1)} %bitcast.3, bf16[1,128,256]{2,1,0:T(8,128)(2,1)} %expand_hbm.1, ...), custom_call_target="tpu_custom_call" | custom-call | tf_op jit(solution)/shard_map/pallas_call | solution.py:565
  41.8 1.4 %copy.13 = bf16[1,12,8,256]{3,2,1,0:T(8,128)(2,1)} copy(bf16[1,12,8,256]{3,2,1,0:T(8,128)(2,1)} %shard_map.109) | data formatting | bytes 98304

commit v3 on v2

v3 whole, which is shorter than its diff:
```python
import functools
import math

import jax
import jax.numpy as jnp
from jax import lax
from jax.experimental import pallas as pl
from jax.experimental.pallas import tpu as pltpu
from jax.sharding import PartitionSpec as P

sigma_data = 0.5
sigma_high = 2.0
sigma_low = 0.5

MESH = pl.DeviceIdType.MESH
bf16 = jnp.bfloat16
f32 = jnp.float32

HALO = 4


def precondition(sigma):
    total = sigma * sigma + sigma_data * sigma_data
    return (
        1.0 / math.sqrt(total),
        sigma_data * sigma_data / total,
        sigma * sigma_data / math.sqrt(total),
        math.log(sigma) / 4.0,
    )


def silu(x):
    half = 0.5 * x
    return half + half * jnp.tanh(half)


def dot(a, b):
    return jnp.dot(a, b, preferred_element_type=f32)


def dot_nt(a, b):
    return lax.dot_general(a, b, (((1,), (1,)), ((), ())), preferred_element_type=f32)


def kernel(
    n_lat,
    n_lon,
    start_hbm,
    prior_hbm,
    lift_w_hbm,
    gain_hbm,
    conv0a,
    expand_hbm,
    conv1a,
    conv1b,
    shrink_hbm,
    conv0b,
    head_hbm,
    out,
    start,
    prior,
    lift_w,
    gain,
    expand,
    shrink,
    head,
    w0a,
    w0b,
    w1a,
    w1b,
    wlift,
    whead,
    outbox,
    inbox,
    rims_out,
    rims_in,
    edges_out,
    edges_in,
    given_t,
    moved,
    shift,
    cells,
    lifted,
    first,
    widened,
    inner,
    merged,
    last,
    finished,
    arrived,
    osem,
    wsem,
    box_s,
    box_r,
    rim_s,
    rim_r,
    edge_s,
    edge_r,
    swap_s,
    swap_r,
):
    section = lax.axis_index("section")
    lat = lax.axis_index("lat")
    lon = lax.axis_index("lon")
    diffuse = section == 1
    variables, rows, cols = prior.shape
    c0 = lift_w.shape[-1]
    half = cols // 2
    own = half // n_lat
    wide = own + 2 * HALO
    slab = widened.shape[2]
    pairs = rows // 2
    total = n_lat * pairs
    used = variables * rows
    lanes = given_t.shape[1]
    high = precondition(sigma_high)
    low = precondition(sigma_low)
    east = lax.rem(lon + 1, n_lon)
    west = lax.rem(lon + n_lon - 1, n_lon)
    final = n_lat - 1

    small = [
        pltpu.make_async_copy(source, landing, osem.at[k])
        for k, (source, landing) in enumerate(
            (
                (start_hbm.at[0], start),
                (prior_hbm, prior),
                (lift_w_hbm.at[0], lift_w),
                (gain_hbm, gain),
                (head_hbm.at[0], head),
                (expand_hbm.at[0], expand),
                (shrink_hbm.at[0], shrink),
            )
        )
    ]
    for copy in small:
        copy.start()

    barrier = pltpu.get_barrier_semaphore()

    def greet(device):
        pl.semaphore_signal(barrier, inc=1, device_id=device, device_id_type=MESH)

    for step in range(1, n_lat):
        greet((section, lax.rem(lat + step, n_lat), lon))
    for k in range(n_lat):
        greet((1 - section, k, lon))

    @pl.when(lat == 0)
    def _():
        for k in range(n_lat):
            greet((section, k, west))

    @pl.when(lat == final)
    def _():
        for k in range(n_lat):
            greet((section, k, east))

    copies = [
        pltpu.make_async_copy(
            conv0a.at[0], w0a.at[pl.ds(0, 3), :, :, pl.ds(0, c0)], wsem.at[0]
        ),
        pltpu.make_async_copy(
            conv0a.at[0], w0a.at[pl.ds(1, 3), :, :, pl.ds(c0, c0)], wsem.at[1]
        ),
        pltpu.make_async_copy(conv1a.at[0], w1a, wsem.at[2]),
        pltpu.make_async_copy(conv1b.at[0], w1b, wsem.at[3]),
        pltpu.make_async_copy(
            conv0b.at[0], w0b.at[pl.ds(0, 3), :, :, pl.ds(0, c0)], wsem.at[4]
        ),
        pltpu.make_async_copy(
            conv0b.at[0], w0b.at[pl.ds(1, 3), :, :, pl.ds(c0, c0)], wsem.at[5]
        ),
    ]
    for copy in copies:
        copy.start()
    for folded in (w0a, w0b):
        blank = jnp.zeros((3, c0, c0), bf16)
        folded[3, :, :, 0:c0] = blank
        folded[0, :, :, c0 : 2 * c0] = blank
    for padded in (lifted, widened, inner, merged):
        blank = jnp.zeros((3,) + padded.shape[2:], bf16)
        padded[:, 0] = blank
        padded[:, total + 1] = blank

    def pick(base, count, parity):
        i = lax.broadcasted_iota(jnp.int32, (count, cols), 0)
        j = lax.broadcasted_iota(jnp.int32, (count, cols), 1)
        return jnp.where(j == 2 * (base + i) + parity, 1.0, 0.0)

    picks = [pick(k * own - HALO, wide, parity) for k in range(n_lat) for parity in range(2)]
    rim_picks = [
        pick(base, 2 * HALO, parity) for base in (half - HALO, -HALO) for parity in range(2)
    ]
    order = jnp.concatenate(picks + rim_picks, axis=0).astype(bf16)

    def turned(x):
        flat = x.reshape(used, cols)
        if lanes > used:
            flat = jnp.concatenate([flat, jnp.zeros((lanes - used, cols), f32)], axis=0)
        return dot_nt(order, flat.astype(bf16))

    small[0].wait()
    small[1].wait()
    full = jnp.concatenate(
        [turned(start[...].astype(f32)), turned(prior[...].astype(f32))], axis=1
    ).astype(bf16)
    for k in range(n_lat):
        outbox[k] = full[2 * wide * k : 2 * wide * (k + 1)]
    for side in range(2):
        at = 2 * wide * n_lat + 4 * HALO * side
        rims_out[side] = full[at : at + 4 * HALO]

    pl.semaphore_wait(barrier, 2 * n_lat + 1)

    def rim(side, source):
        return pltpu.make_async_remote_copy(
            src_ref=rims_out.at[side],
            dst_ref=rims_in.at[side, source],
            send_sem=rim_s.at[side],
            recv_sem=rim_r.at[side, source],
            device_id=(section, 0, east) if side == 0 else (section, final, west),
            device_id_type=MESH,
        )

    def box(step, source):
        to = lax.rem(lat + step, n_lat)
        return pltpu.make_async_remote_copy(
            src_ref=outbox.at[to],
            dst_ref=inbox.at[source],
            send_sem=box_s.at[step - 1],
            recv_sem=box_r.at[step - 1],
            device_id=(section, to, lon),
            device_id_type=MESH,
        )

    for side in range(2):
        rim(side, lat).start()
    for step in range(1, n_lat):
        box(step, lat).start()
    inbox[lat] = outbox[lat]

    for copy in small[2:]:
        copy.wait()
    spread_w = jnp.broadcast_to(
        lift_w[...].astype(f32)[:, None, :], (2 * variables, rows, c0)
    ).reshape(2 * used, c0)
    row_of = lax.rem(lax.broadcasted_iota(jnp.int32, (lanes, c0), 0), rows)
    for part in range(2):
        piece = spread_w[part * used : (part + 1) * used]
        if lanes > used:
            piece = jnp.concatenate([piece, jnp.zeros((lanes - used, c0), f32)], axis=0)
        for r in range(rows):
            wlift[
                r // 2, part * lanes : (part + 1) * lanes, (r % 2) * c0 : (r % 2 + 1) * c0
            ] = jnp.where(row_of == r, piece, 0.0).astype(bf16)
    v_id = lax.broadcasted_iota(jnp.int32, (variables, lanes), 0)
    l_id = lax.broadcasted_iota(jnp.int32, (variables, lanes), 1)
    spreading = jnp.where((l_id >= v_id * rows) & (l_id < (v_id + 1) * rows), 1.0, 0.0).astype(bf16)
    spread_h = lax.dot_general(
        head[...], spreading, (((0,), (0,)), ((), ())), preferred_element_type=f32
    )
    lane_row = lax.rem(lax.broadcasted_iota(jnp.int32, (c0, lanes), 1), rows)
    for r in range(rows):
        whead[r * c0 : (r + 1) * c0, :] = jnp.where(lane_row == r, spread_h, 0.0).astype(bf16)
    expand_w = expand[...]
    shrink_w = jnp.concatenate([shrink[...], shrink[...]], axis=1)
    gains = jnp.concatenate([gain[...], gain[...]], axis=1)
    shift[...] = jnp.where(diffuse, high[3], 0.0).astype(f32) * gains

    for step in range(1, n_lat):
        box(step, lax.rem(lat + n_lat - step, n_lat)).wait_recv()

    @pl.when(lat == 0)
    def _():
        for k in range(n_lat):
            rim(0, k).wait_recv()

    @pl.when(lat == final)
    def _():
        for k in range(n_lat):
            rim(1, k).wait_recv()

    scale = jnp.where(diffuse, high[0] * sigma_high, 1.0).astype(f32)
    near = lax.broadcasted_iota(jnp.int32, (2 * HALO, lanes), 0) < HALO
    depth = 2 * HALO
    for k in range(n_lat):
        block = inbox[k].astype(f32)
        left = jnp.where(lat == 0, rims_in[0, k].astype(f32), 0.0)
        right = jnp.where(lat == final, rims_in[1, k].astype(f32), 0.0)
        whole = []
        for parity in range(2):
            part = block[parity * wide : (parity + 1) * wide]
            rim_rows = slice(parity * depth, (parity + 1) * depth)
            whole += [
                part[:depth] + left[rim_rows],
                part[depth : wide - depth],
                part[wide - depth :] + right[rim_rows],
            ]
        whole = jnp.concatenate(whole, axis=0)
        place = slice(2 * wide * k, 2 * wide * (k + 1))
        given_t[place] = whole[:, :lanes]
        cells[place, :lanes] = (scale * whole[:, :lanes]).astype(bf16)
        cells[place, lanes:] = whole[:, lanes:].astype(bf16)

    def keep_fine(buffer, index, value):
        even, odd = value[:wide], value[wide:]
        buffer[0, index] = jnp.concatenate([pltpu.roll(odd, 1, 0), even], axis=0).astype(bf16)
        buffer[1, index] = value.astype(bf16)
        buffer[2, index] = jnp.concatenate(
            [odd, pltpu.roll(even, wide - 1, 0)], axis=0
        ).astype(bf16)

    def keep_coarse(buffer, index, value):
        buffer[0, index] = pltpu.roll(value, 1, 0).astype(bf16)
        buffer[1, index] = value.astype(bf16)
        buffer[2, index] = pltpu.roll(value, slab - 1, 0).astype(bf16)

    def fine_window(buffer, index):
        pieces = []
        for at, lane in ((0, c0), (1, 0), (1, c0), (2, 0)):
            pieces += [buffer[b, index + at, :, lane : lane + c0] for b in range(3)]
        return jnp.concatenate(pieces, axis=1)

    def coarse_window(buffer, index):
        return jnp.concatenate(
            [buffer[b, index + a] for a in range(3) for b in range(3)], axis=1
        )

    def stacked(window, buffer, indices):
        return jnp.concatenate([window(buffer, index) for index in indices], axis=0)

    def groups(count):
        return [range(at, at + count) for at in range(0, total, count)]

    def network(loading):
        for p in range(pairs):
            value = silu(dot(cells[...], wlift[p]) + shift[...])
            for k in range(n_lat):
                keep_fine(
                    lifted, k * pairs + p + 1, value[2 * wide * k : 2 * wide * (k + 1)]
                )
        if loading:
            copies[0].wait()
            copies[1].wait()
        for group in groups(pairs):
            acc = dot(stacked(fine_window, lifted, group), w0a[...].reshape(12 * c0, 2 * c0))
            value = silu(acc).astype(bf16)
            pooled = []
            for k, index in enumerate(group):
                piece = value[2 * wide * k : 2 * wide * (k + 1)]
                first[index] = piece
                piece = piece.astype(f32)
                piece = piece[:wide] + piece[wide:]
                pooled.append((piece[:, :c0] + piece[:, c0:]) * 0.25)
                if slab > wide:
                    pooled.append(jnp.zeros((slab - wide, c0), f32))
            result = dot(jnp.concatenate(pooled, axis=0).astype(bf16), expand_w)
            for k, index in enumerate(group):
                keep_coarse(widened, index + 1, result[slab * k : slab * (k + 1)])
        if loading:
            copies[2].wait()
        for group in groups(2 * pairs):
            acc = dot(
                stacked(coarse_window, widened, group),
                w1a[...].reshape(9 * w1a.shape[1], w1a.shape[2]),
            )
            value = silu(acc)
            for k, index in enumerate(group):
                keep_coarse(inner, index + 1, value[slab * k : slab * (k + 1)])
        if loading:
            copies[3].wait()
        for group in groups(2 * pairs):
            acc = dot(
                stacked(coarse_window, inner, group),
                w1b[...].reshape(9 * w1b.shape[1], w1b.shape[2]),
            )
            skip = jnp.concatenate([widened[1, index + 1] for index in group], axis=0)
            projected = dot((silu(acc) + skip.astype(f32)).astype(bf16), shrink_w)
            for k, index in enumerate(group):
                piece = projected[slab * k : slab * k + wide]
                keep_fine(
                    merged,
                    index + 1,
                    jnp.concatenate([piece, piece], axis=0) + first[index].astype(f32),
                )
        if loading:
            copies[4].wait()
            copies[5].wait()
        for group in groups(pairs):
            acc = dot(stacked(fine_window, merged, group), w0b[...].reshape(12 * c0, 2 * c0))
            value = silu(acc).astype(bf16)
            for k, index in enumerate(group):
                last[index] = value[2 * wide * k : 2 * wide * (k + 1)]
        return dot(
            jnp.concatenate(
                [
                    jnp.concatenate([last[index] for index in group], axis=1)
                    for group in groups(pairs)
                ],
                axis=0,
            ),
            whead[...],
        )

    def swap(to, source):
        return pltpu.make_async_remote_copy(
            src_ref=finished.at[to],
            dst_ref=arrived.at[source],
            send_sem=swap_s.at[to],
            recv_sem=swap_r.at[source],
            device_id=(1 - section, to, lon),
            device_id_type=MESH,
        )

    def hand_over(value):
        value = value.astype(bf16)
        for k in range(n_lat):
            finished[k] = value[2 * wide * k : 2 * wide * (k + 1)]
        for k in range(n_lat):
            swap(k, lat).start()

    first_out = network(True)
    for side in range(2):
        rim(side, lat).wait_send()
    for step in range(1, n_lat):
        box(step, lat).wait_send()

    @pl.when(jnp.logical_not(diffuse))
    def _():
        hand_over(first_out)

    @pl.when(diffuse)
    def _():
        noisy = sigma_high * given_t[...]
        first_denoised = high[1] * noisy + high[2] * first_out
        fresh = noisy + (sigma_low - sigma_high) / sigma_high * (noisy - first_denoised)
        moved[...] = fresh
        second_input = low[0] * fresh

        def part(k, parity):
            at = 2 * wide * k + wide * parity
            return second_input[at : at + wide]

        order_of = [(k, parity) for k in range(n_lat) for parity in range(2)]
        edges_out[0] = jnp.concatenate(
            [part(*at)[wide - depth :] for at in order_of], axis=0
        ).astype(bf16)
        edges_out[1] = jnp.concatenate([part(*at)[:depth] for at in order_of], axis=0).astype(bf16)

        to_east = (
            section,
            lax.rem(lat + 1, n_lat),
            lax.rem(lon + jnp.where(lat == final, 1, 0), n_lon),
        )
        to_west = (
            section,
            lax.rem(lat + n_lat - 1, n_lat),
            lax.rem(lon + n_lon - jnp.where(lat == 0, 1, 0), n_lon),
        )
        edges = [
            pltpu.make_async_remote_copy(
                src_ref=edges_out.at[side],
                dst_ref=edges_in.at[side],
                send_sem=edge_s.at[side],
                recv_sem=edge_r.at[side],
                device_id=(to_east, to_west)[side],
                device_id_type=MESH,
            )
            for side in range(2)
        ]
        for edge in edges:
            edge.start()
        shift[...] = low[3] * gains
        for edge in edges:
            edge.wait_recv()
        left = edges_in[0].astype(f32)
        right = edges_in[1].astype(f32)
        whole = []
        for n, at in enumerate(order_of):
            piece = part(*at)
            rim_rows = slice(depth * n, depth * (n + 1))
            whole += [
                jnp.where(near, left[rim_rows], piece[:depth]),
                piece[depth : wide - depth],
                jnp.where(near, piece[wide - depth :], right[rim_rows]),
            ]
        cells[:, :lanes] = jnp.concatenate(whole, axis=0).astype(bf16)
        second_out = network(False)
        second_denoised = low[1] * moved[...] + low[2] * second_out
        hand_over(cells[:, lanes:].astype(f32) + second_denoised)
        for edge in edges:
            edge.wait_send()

    def unpick(base):
        i = lax.broadcasted_iota(jnp.int32, (wide, cols), 0)
        j = lax.broadcasted_iota(jnp.int32, (wide, cols), 1)
        middle = (i >= HALO) & (i < wide - HALO)
        return [
            jnp.where(middle & (j == 2 * (base + i) + parity), 1.0, 0.0) for parity in range(2)
        ]

    back = jnp.concatenate(
        [piece for k in range(n_lat) for piece in unpick(k * own - HALO)], axis=0
    ).astype(bf16)
    a = lax.broadcasted_iota(jnp.int32, (lanes, lanes), 0)
    b = lax.broadcasted_iota(jnp.int32, (lanes, lanes), 1)
    eye = jnp.where(a == b, 1.0, 0.0).astype(bf16)
    for k in range(n_lat):
        swap(k, k).wait_recv()
    gathered = arrived[...].reshape(n_lat * 2 * wide, lanes)
    result = dot(dot_nt(eye, gathered).astype(bf16), back)[:used]
    out[0] = result.reshape(variables, rows, cols).astype(bf16)
    for k in range(n_lat):
        swap(k, lat).wait_send()


def on_device(
    n_lat,
    n_lon,
    start,
    prior_mean,
    lift_w,
    noise_gain,
    conv0a,
    expand,
    conv1a,
    conv1b,
    shrink,
    conv0b,
    head,
):
    variables, rows, cols = prior_mean.shape
    c0, c1 = expand.shape[1:]
    pairs = rows // 2
    total = n_lat * pairs
    wide = cols // 2 // n_lat + 2 * HALO
    slab = -(-wide // 16) * 16
    used = variables * rows
    lanes = -(-used // 128) * 128
    depth = 4 * HALO
    assert 2 * c0 == c1 and wide % 8 == 0 and n_lat % 2 == 0 and rows % 2 == 0
    split = (1, 3, 3, c0, c0)
    head_t = jnp.swapaxes(head, 1, 2)
    scratch = [
        pltpu.VMEM(start.shape[1:], bf16),
        pltpu.VMEM(prior_mean.shape, bf16),
        pltpu.VMEM(lift_w.shape[1:], bf16),
        pltpu.VMEM(noise_gain.shape, f32),
        pltpu.VMEM(expand.shape[1:], bf16),
        pltpu.VMEM(shrink.shape[1:], bf16),
        pltpu.VMEM(head_t.shape[1:], bf16),
        pltpu.VMEM((4, 3, c0, 2 * c0), bf16),
        pltpu.VMEM((4, 3, c0, 2 * c0), bf16),
        pltpu.VMEM((9, c1, c1), bf16),
        pltpu.VMEM((9, c1, c1), bf16),
        pltpu.VMEM((pairs, 2 * lanes, 2 * c0), bf16),
        pltpu.VMEM((rows * c0, lanes), bf16),
        pltpu.VMEM((n_lat, 2 * wide, 2 * lanes), bf16),
        pltpu.VMEM((n_lat, 2 * wide, 2 * lanes), bf16),
        pltpu.VMEM((2, depth, 2 * lanes), bf16),
        pltpu.VMEM((2, n_lat, depth, 2 * lanes), bf16),
        pltpu.VMEM((2, n_lat * depth, lanes), bf16),
        pltpu.VMEM((2, n_lat * depth, lanes), bf16),
        pltpu.VMEM((n_lat * 2 * wide, lanes), f32),
        pltpu.VMEM((n_lat * 2 * wide, lanes), f32),
        pltpu.VMEM((1, 2 * c0), f32),
        pltpu.VMEM((n_lat * 2 * wide, 2 * lanes), bf16),
        pltpu.VMEM((3, total + 2, 2 * wide, 2 * c0), bf16),
        pltpu.VMEM((total, 2 * wide, 2 * c0), bf16),
        pltpu.VMEM((3, total + 2, slab, c1), bf16),
        pltpu.VMEM((3, total + 2, slab, c1), bf16),
        pltpu.VMEM((3, total + 2, 2 * wide, 2 * c0), bf16),
        pltpu.VMEM((total, 2 * wide, 2 * c0), bf16),
        pltpu.VMEM((n_lat, 2 * wide, lanes), bf16),
        pltpu.VMEM((n_lat, 2 * wide, lanes), bf16),
        pltpu.SemaphoreType.DMA((7,)),
        pltpu.SemaphoreType.DMA((6,)),
        pltpu.SemaphoreType.DMA((n_lat - 1,)),
        pltpu.SemaphoreType.DMA((n_lat - 1,)),
        pltpu.SemaphoreType.DMA((2,)),
        pltpu.SemaphoreType.DMA((2, n_lat)),
        pltpu.SemaphoreType.DMA((2,)),
        pltpu.SemaphoreType.DMA((2,)),
        pltpu.SemaphoreType.DMA((n_lat,)),
        pltpu.SemaphoreType.DMA((n_lat,)),
    ]
    return pl.pallas_call(
        functools.partial(kernel, n_lat, n_lon),
        out_shape=jax.ShapeDtypeStruct((1, variables, rows, cols), bf16),
        in_specs=[pl.BlockSpec(memory_space=pl.ANY)] * 11,
        out_specs=pl.BlockSpec(memory_space=pltpu.VMEM),
        scratch_shapes=scratch,
        compiler_params=pltpu.CompilerParams(
            collective_id=0, has_side_effects=True, vmem_limit_bytes=60 * 2**20
        ),
    )(
        start,
        prior_mean,
        lift_w,
        noise_gain,
        conv0a.reshape(split),
        expand,
        conv1a,
        conv1b,
        shrink,
        conv0b.reshape(split),
        head_t,
    )


def solution(mesh):
    placed = (
        P("section", None, "lat", "lon"),
        P(None, "lat", "lon"),
        P("section", None, None),
        P("section", None),
        P("section", None, None, None),
        P("section", None, None),
        P("section", None, None, None),
        P("section", None, None, None),
        P("section", None, None),
        P("section", None, None, None),
        P("section", None, None),
    )
    return jax.shard_map(
        functools.partial(on_device, mesh.shape["lat"], mesh.shape["lon"]),
        mesh=mesh,
        in_specs=placed,
        out_specs=P("section", None, "lat", "lon"),
        check_vma=False,
    )
```

time: 43.4 us -> 34.8 us (0.80)
  Pallas kernels: 41.8 us -> 33.2 us
    pallas_call x1, Pallas kernels: 41.8 us -> 33.2 us  [on_device(): pl.pallas_call(functools.partial(kernel, n_lat, n_lon), out_shape=jax.Sha...]
where the time goes in v3:
time: 34.8 us; the launch traced here: 34.6 us
  Pallas kernels  33.2 us (95%)
  local copies, waits for them, and re-layouts  1.42 us (4%)
    pallas_call x1, Pallas kernels, on_device(): pl.pallas_call(functools.partial(kernel, n_lat, n_lon), out_shape=jax.Sha...  33.2 us
    unnamed x1, local copies, waits for them, and re-layouts  1.42 us

profile of v3, /device:TPU:0, one launch (start us, length us, event | category | flops | bytes accessed | tf_op | source)
XLA Modules:
  0.0 34.6 jit_solution(14568799791585926484)
XLA Ops:
  0.0 33.2 %shard_map.109 = bf16[1,12,8,256]{3,2,1,0:T(8,128)(2,1)} custom-call(bf16[1,12,8,256]{3,2,1,0:T(8,128)(2,1)} %start_hbm.1, bf16[12,8,256]{2,1,0:T(8,128)(2,1)} %prior_hbm.1, bf16[1,24,128]{2,1,0:T(8,128)(2,1)} %lift_w_hbm.1, f32[1,128]{1,0:T(1,128)} %gain_hbm.1, bf16[1,3,3,128,128]{4,3,2,1,0:T(8,128)(2,1)} %bitcast.3, bf16[1,128,256]{2,1,0:T(8,128)(2,1)} %expand_hbm.1, ...), custom_call_target="tpu_custom_call" | custom-call | tf_op jit(solution)/shard_map/pallas_call | solution.py:588
  33.2 1.4 %copy.13 = bf16[1,12,8,256]{3,2,1,0:T(8,128)(2,1)} copy(bf16[1,12,8,256]{3,2,1,0:T(8,128)(2,1)} %shard_map.109) | data formatting | bytes 98304

commit v4 on v3

--- a/solution.py
+++ b/solution.py
@@ -343,7 +343,7 @@
         if loading:
             copies[0].wait()
             copies[1].wait()
-        for group in groups(pairs):
+        for group in groups(total):
             acc = dot(stacked(fine_window, lifted, group), w0a[...].reshape(12 * c0, 2 * c0))
             value = silu(acc).astype(bf16)
             pooled = []
@@ -360,7 +360,7 @@
                 keep_coarse(widened, index + 1, result[slab * k : slab * (k + 1)])
         if loading:
             copies[2].wait()
-        for group in groups(2 * pairs):
+        for group in groups(total):
             acc = dot(
                 stacked(coarse_window, widened, group),
                 w1a[...].reshape(9 * w1a.shape[1], w1a.shape[2]),
@@ -370,7 +370,7 @@
                 keep_coarse(inner, index + 1, value[slab * k : slab * (k + 1)])
         if loading:
             copies[3].wait()
-        for group in groups(2 * pairs):
+        for group in groups(total):
             acc = dot(
                 stacked(coarse_window, inner, group),
                 w1b[...].reshape(9 * w1b.shape[1], w1b.shape[2]),
@@ -387,7 +387,7 @@
         if loading:
             copies[4].wait()
             copies[5].wait()
-        for group in groups(pairs):
+        for group in groups(total):
             acc = dot(stacked(fine_window, merged, group), w0b[...].reshape(12 * c0, 2 * c0))
             value = silu(acc).astype(bf16)
             for k, index in enumerate(group):

time: 34.8 us -> 37.9 us (1.089)
  Pallas kernels: 33.2 us -> 36.3 us
    pallas_call x1, Pallas kernels: 33.2 us -> 36.3 us  [on_device(): pl.pallas_call(functools.partial(kernel, n_lat, n_lon), out_shape=jax.Sha...]
where the time goes in v4:
time: 37.9 us; the launch traced here: 37.7 us
  Pallas kernels  36.3 us (96%)
  local copies, waits for them, and re-layouts  1.42 us (4%)
    pallas_call x1, Pallas kernels, on_device(): pl.pallas_call(functools.partial(kernel, n_lat, n_lon), out_shape=jax.Sha...  36.3 us
    unnamed x1, local copies, waits for them, and re-layouts  1.42 us

profile of v4, /device:TPU:0, one launch (start us, length us, event | category | flops | bytes accessed | tf_op | source)
XLA Modules:
  0.0 37.7 jit_solution(12021712875778275171)
XLA Ops:
  0.0 36.3 %shard_map.109 = bf16[1,12,8,256]{3,2,1,0:T(8,128)(2,1)} custom-call(bf16[1,12,8,256]{3,2,1,0:T(8,128)(2,1)} %start_hbm.1, bf16[12,8,256]{2,1,0:T(8,128)(2,1)} %prior_hbm.1, bf16[1,24,128]{2,1,0:T(8,128)(2,1)} %lift_w_hbm.1, f32[1,128]{1,0:T(1,128)} %gain_hbm.1, bf16[1,3,3,128,128]{4,3,2,1,0:T(8,128)(2,1)} %bitcast.3, bf16[1,128,256]{2,1,0:T(8,128)(2,1)} %expand_hbm.1, ...), custom_call_target="tpu_custom_call" | custom-call | tf_op jit(solution)/shard_map/pallas_call | solution.py:588
  36.3 1.4 %copy.13 = bf16[1,12,8,256]{3,2,1,0:T(8,128)(2,1)} copy(bf16[1,12,8,256]{3,2,1,0:T(8,128)(2,1)} %shard_map.109) | data formatting | bytes 98304

commit v5 on v4

--- a/solution.py
+++ b/solution.py
@@ -343,7 +343,7 @@
         if loading:
             copies[0].wait()
             copies[1].wait()
-        for group in groups(total):
+        for group in groups(pairs // 2):
             acc = dot(stacked(fine_window, lifted, group), w0a[...].reshape(12 * c0, 2 * c0))
             value = silu(acc).astype(bf16)
             pooled = []
@@ -360,7 +360,7 @@
                 keep_coarse(widened, index + 1, result[slab * k : slab * (k + 1)])
         if loading:
             copies[2].wait()
-        for group in groups(total):
+        for group in groups(pairs):
             acc = dot(
                 stacked(coarse_window, widened, group),
                 w1a[...].reshape(9 * w1a.shape[1], w1a.shape[2]),
@@ -370,7 +370,7 @@
                 keep_coarse(inner, index + 1, value[slab * k : slab * (k + 1)])
         if loading:
             copies[3].wait()
-        for group in groups(total):
+        for group in groups(pairs):
             acc = dot(
                 stacked(coarse_window, inner, group),
                 w1b[...].reshape(9 * w1b.shape[1], w1b.shape[2]),
@@ -387,7 +387,7 @@
         if loading:
             copies[4].wait()
             copies[5].wait()
-        for group in groups(total):
+        for group in groups(pairs // 2):
             acc = dot(stacked(fine_window, merged, group), w0b[...].reshape(12 * c0, 2 * c0))
             value = silu(acc).astype(bf16)
             for k, index in enumerate(group):

time: 37.9 us -> 36.5 us (0.963)
  Pallas kernels: 36.3 us -> 34.9 us
    pallas_call x1, Pallas kernels: 36.3 us -> 34.9 us  [on_device(): pl.pallas_call(functools.partial(kernel, n_lat, n_lon), out_shape=jax.Sha...]
where the time goes in v5:
time: 36.5 us; the launch traced here: 36.3 us
  Pallas kernels  34.9 us (96%)
  local copies, waits for them, and re-layouts  1.42 us (4%)
    pallas_call x1, Pallas kernels, on_device(): pl.pallas_call(functools.partial(kernel, n_lat, n_lon), out_shape=jax.Sha...  34.9 us
    unnamed x1, local copies, waits for them, and re-layouts  1.42 us

profile of v5, /device:TPU:0, one launch (start us, length us, event | category | flops | bytes accessed | tf_op | source)
XLA Modules:
  0.0 36.3 jit_solution(8821940219773617103)
XLA Ops:
  0.0 34.9 %shard_map.109 = bf16[1,12,8,256]{3,2,1,0:T(8,128)(2,1)} custom-call(bf16[1,12,8,256]{3,2,1,0:T(8,128)(2,1)} %start_hbm.1, bf16[12,8,256]{2,1,0:T(8,128)(2,1)} %prior_hbm.1, bf16[1,24,128]{2,1,0:T(8,128)(2,1)} %lift_w_hbm.1, f32[1,128]{1,0:T(1,128)} %gain_hbm.1, bf16[1,3,3,128,128]{4,3,2,1,0:T(8,128)(2,1)} %bitcast.3, bf16[1,128,256]{2,1,0:T(8,128)(2,1)} %expand_hbm.1, ...), custom_call_target="tpu_custom_call" | custom-call | tf_op jit(solution)/shard_map/pallas_call | solution.py:588
  34.9 1.4 %copy.13 = bf16[1,12,8,256]{3,2,1,0:T(8,128)(2,1)} copy(bf16[1,12,8,256]{3,2,1,0:T(8,128)(2,1)} %shard_map.109) | data formatting | bytes 98304

commit v6 on v3

--- a/solution.py
+++ b/solution.py
@@ -17,6 +17,7 @@
 f32 = jnp.float32
 
 HALO = 4
+RIM = 2 * HALO
 
 
 def precondition(sigma):
@@ -74,9 +75,8 @@
     inbox,
     rims_out,
     rims_in,
-    edges_out,
-    edges_in,
     given_t,
+    prior_t,
     moved,
     shift,
     cells,
@@ -94,8 +94,6 @@
     box_r,
     rim_s,
     rim_r,
-    edge_s,
-    edge_r,
     swap_s,
     swap_r,
 ):
@@ -107,7 +105,7 @@
     c0 = lift_w.shape[-1]
     half = cols // 2
     own = half // n_lat
-    wide = own + 2 * HALO
+    broad = own + 2 * RIM
     slab = widened.shape[2]
     pairs = rows // 2
     total = n_lat * pairs
@@ -174,24 +172,13 @@
     ]
     for copy in copies:
         copy.start()
-    for folded in (w0a, w0b):
-        blank = jnp.zeros((3, c0, c0), bf16)
-        folded[3, :, :, 0:c0] = blank
-        folded[0, :, :, c0 : 2 * c0] = blank
-    for padded in (lifted, widened, inner, merged):
-        blank = jnp.zeros((3,) + padded.shape[2:], bf16)
-        padded[:, 0] = blank
-        padded[:, total + 1] = blank
-
     def pick(base, count, parity):
         i = lax.broadcasted_iota(jnp.int32, (count, cols), 0)
         j = lax.broadcasted_iota(jnp.int32, (count, cols), 1)
         return jnp.where(j == 2 * (base + i) + parity, 1.0, 0.0)
 
-    picks = [pick(k * own - HALO, wide, parity) for k in range(n_lat) for parity in range(2)]
-    rim_picks = [
-        pick(base, 2 * HALO, parity) for base in (half - HALO, -HALO) for parity in range(2)
-    ]
+    picks = [pick(k * own - RIM, broad, parity) for k in range(n_lat) for parity in range(2)]
+    rim_picks = [pick(base, RIM, parity) for base in (half - RIM, 0) for parity in range(2)]
     order = jnp.concatenate(picks + rim_picks, axis=0).astype(bf16)
 
     def turned(x):
@@ -206,10 +193,10 @@
         [turned(start[...].astype(f32)), turned(prior[...].astype(f32))], axis=1
     ).astype(bf16)
     for k in range(n_lat):
-        outbox[k] = full[2 * wide * k : 2 * wide * (k + 1)]
+        outbox[k] = full[2 * broad * k : 2 * broad * (k + 1)]
     for side in range(2):
-        at = 2 * wide * n_lat + 4 * HALO * side
-        rims_out[side] = full[at : at + 4 * HALO]
+        at = 2 * broad * n_lat + 2 * RIM * side
+        rims_out[side] = full[at : at + 2 * RIM]
 
     pl.semaphore_wait(barrier, 2 * n_lat + 1)
 
@@ -239,6 +226,15 @@
     for step in range(1, n_lat):
         box(step, lat).start()
     inbox[lat] = outbox[lat]
+
+    for folded in (w0a, w0b):
+        blank = jnp.zeros((3, c0, c0), bf16)
+        folded[3, :, :, 0:c0] = blank
+        folded[0, :, :, c0 : 2 * c0] = blank
+    for padded in (lifted, widened, inner, merged):
+        blank = jnp.zeros((3,) + padded.shape[2:], bf16)
+        padded[:, 0] = blank
+        padded[:, total + 1] = blank
 
     for copy in small[2:]:
         copy.wait()
@@ -282,32 +278,35 @@
             rim(1, k).wait_recv()
 
     scale = jnp.where(diffuse, high[0] * sigma_high, 1.0).astype(f32)
-    near = lax.broadcasted_iota(jnp.int32, (2 * HALO, lanes), 0) < HALO
-    depth = 2 * HALO
     for k in range(n_lat):
         block = inbox[k].astype(f32)
         left = jnp.where(lat == 0, rims_in[0, k].astype(f32), 0.0)
         right = jnp.where(lat == final, rims_in[1, k].astype(f32), 0.0)
         whole = []
         for parity in range(2):
-            part = block[parity * wide : (parity + 1) * wide]
-            rim_rows = slice(parity * depth, (parity + 1) * depth)
+            part = block[parity * broad : (parity + 1) * broad]
+            rim_rows = slice(parity * RIM, (parity + 1) * RIM)
             whole += [
-                part[:depth] + left[rim_rows],
-                part[depth : wide - depth],
-                part[wide - depth :] + right[rim_rows],
+                part[:RIM] + left[rim_rows],
+                part[RIM : broad - RIM],
+                part[broad - RIM :] + right[rim_rows],
             ]
         whole = jnp.concatenate(whole, axis=0)
-        place = slice(2 * wide * k, 2 * wide * (k + 1))
+        place = slice(2 * broad * k, 2 * broad * (k + 1))
         given_t[place] = whole[:, :lanes]
+        prior_t[place] = whole[:, lanes:]
         cells[place, :lanes] = (scale * whole[:, :lanes]).astype(bf16)
         cells[place, lanes:] = whole[:, lanes:].astype(bf16)
 
     def keep_fine(buffer, index, value):
+        wide = value.shape[0] // 2
         even, odd = value[:wide], value[wide:]
-        buffer[0, index] = jnp.concatenate([pltpu.roll(odd, 1, 0), even], axis=0).astype(bf16)
-        buffer[1, index] = value.astype(bf16)
-        buffer[2, index] = jnp.concatenate(
+        place = slice(0, 2 * wide)
+        buffer[0, index, place] = jnp.concatenate([pltpu.roll(odd, 1, 0), even], axis=0).astype(
+            bf16
+        )
+        buffer[1, index, place] = value.astype(bf16)
+        buffer[2, index, place] = jnp.concatenate(
             [odd, pltpu.roll(even, wide - 1, 0)], axis=0
         ).astype(bf16)
 
@@ -316,10 +315,10 @@
         buffer[1, index] = value.astype(bf16)
         buffer[2, index] = pltpu.roll(value, slab - 1, 0).astype(bf16)
 
-    def fine_window(buffer, index):
+    def fine_window(wide, buffer, index):
         pieces = []
         for at, lane in ((0, c0), (1, 0), (1, c0), (2, 0)):
-            pieces += [buffer[b, index + at, :, lane : lane + c0] for b in range(3)]
+            pieces += [buffer[b, index + at, 0 : 2 * wide, lane : lane + c0] for b in range(3)]
         return jnp.concatenate(pieces, axis=1)
 
     def coarse_window(buffer, index):
@@ -333,9 +332,11 @@
     def groups(count):
         return [range(at, at + count) for at in range(0, total, count)]
 
-    def network(loading):
+    def network(loading, wide):
+        fine = functools.partial(fine_window, wide)
+        tall = 2 * wide
         for p in range(pairs):
-            value = silu(dot(cells[...], wlift[p]) + shift[...])
+            value = silu(dot(cells[0 : n_lat * tall], wlift[p]) + shift[...])
             for k in range(n_lat):
                 keep_fine(
                     lifted, k * pairs + p + 1, value[2 * wide * k : 2 * wide * (k + 1)]
@@ -344,12 +345,12 @@
             copies[0].wait()
             copies[1].wait()
         for group in groups(pairs):
-            acc = dot(stacked(fine_window, lifted, group), w0a[...].reshape(12 * c0, 2 * c0))
+            acc = dot(stacked(fine, lifted, group), w0a[...].reshape(12 * c0, 2 * c0))
             value = silu(acc).astype(bf16)
             pooled = []
             for k, index in enumerate(group):
                 piece = value[2 * wide * k : 2 * wide * (k + 1)]
-                first[index] = piece
+                first[index, 0:tall] = piece
                 piece = piece.astype(f32)
                 piece = piece[:wide] + piece[wide:]
                 pooled.append((piece[:, :c0] + piece[:, c0:]) * 0.25)
@@ -382,20 +383,20 @@
                 keep_fine(
                     merged,
                     index + 1,
-                    jnp.concatenate([piece, piece], axis=0) + first[index].astype(f32),
+                    jnp.concatenate([piece, piece], axis=0) + first[index, 0:tall].astype(f32),
                 )
         if loading:
             copies[4].wait()
             copies[5].wait()
         for group in groups(pairs):
-            acc = dot(stacked(fine_window, merged, group), w0b[...].reshape(12 * c0, 2 * c0))
+            acc = dot(stacked(fine, merged, group), w0b[...].reshape(12 * c0, 2 * c0))
             value = silu(acc).astype(bf16)
             for k, index in enumerate(group):
-                last[index] = value[2 * wide * k : 2 * wide * (k + 1)]
+                last[index, 0:tall] = value[2 * wide * k : 2 * wide * (k + 1)]
         return dot(
             jnp.concatenate(
                 [
-                    jnp.concatenate([last[index] for index in group], axis=1)
+                    jnp.concatenate([last[index, 0:tall] for index in group], axis=1)
                     for group in groups(pairs)
                 ],
                 axis=0,
@@ -413,14 +414,18 @@
             device_id_type=MESH,
         )
 
-    def hand_over(value):
-        value = value.astype(bf16)
+    def hand_over(pieces):
         for k in range(n_lat):
-            finished[k] = value[2 * wide * k : 2 * wide * (k + 1)]
+            finished[k] = jnp.concatenate(pieces[2 * k : 2 * k + 2], axis=0).astype(bf16)
         for k in range(n_lat):
             swap(k, lat).start()
 
-    first_out = network(True)
+    def trimmed(ref, size, margin):
+        return [
+            ref[size * n + margin : size * (n + 1) - margin] for n in range(2 * n_lat)
+        ]
+
+    first_out = network(True, broad)
     for side in range(2):
         rim(side, lat).wait_send()
     for step in range(1, n_lat):
@@ -428,87 +433,36 @@
 
     @pl.when(jnp.logical_not(diffuse))
     def _():
-        hand_over(first_out)
+        moved[...] = first_out
+        hand_over(trimmed(moved, broad, RIM))
 
     @pl.when(diffuse)
     def _():
         noisy = sigma_high * given_t[...]
         first_denoised = high[1] * noisy + high[2] * first_out
-        fresh = noisy + (sigma_low - sigma_high) / sigma_high * (noisy - first_denoised)
-        moved[...] = fresh
-        second_input = low[0] * fresh
-
-        def part(k, parity):
-            at = 2 * wide * k + wide * parity
-            return second_input[at : at + wide]
-
-        order_of = [(k, parity) for k in range(n_lat) for parity in range(2)]
-        edges_out[0] = jnp.concatenate(
-            [part(*at)[wide - depth :] for at in order_of], axis=0
-        ).astype(bf16)
-        edges_out[1] = jnp.concatenate([part(*at)[:depth] for at in order_of], axis=0).astype(bf16)
-
-        to_east = (
-            section,
-            lax.rem(lat + 1, n_lat),
-            lax.rem(lon + jnp.where(lat == final, 1, 0), n_lon),
-        )
-        to_west = (
-            section,
-            lax.rem(lat + n_lat - 1, n_lat),
-            lax.rem(lon + n_lon - jnp.where(lat == 0, 1, 0), n_lon),
-        )
-        edges = [
-            pltpu.make_async_remote_copy(
-                src_ref=edges_out.at[side],
-                dst_ref=edges_in.at[side],
-                send_sem=edge_s.at[side],
-                recv_sem=edge_r.at[side],
-                device_id=(to_east, to_west)[side],
-                device_id_type=MESH,
-            )
-            for side in range(2)
-        ]
-        for edge in edges:
-            edge.start()
+        moved[...] = noisy + (sigma_low - sigma_high) / sigma_high * (noisy - first_denoised)
+        wide = broad - 2 * HALO
+        rows_in = slice(0, 2 * n_lat * wide)
+        fresh = jnp.concatenate(trimmed(moved, broad, HALO), axis=0)
+        near_prior = jnp.concatenate(trimmed(prior_t, broad, HALO), axis=0)
+        cells[rows_in, :lanes] = (low[0] * fresh).astype(bf16)
+        cells[rows_in, lanes:] = near_prior.astype(bf16)
         shift[...] = low[3] * gains
-        for edge in edges:
-            edge.wait_recv()
-        left = edges_in[0].astype(f32)
-        right = edges_in[1].astype(f32)
-        whole = []
-        for n, at in enumerate(order_of):
-            piece = part(*at)
-            rim_rows = slice(depth * n, depth * (n + 1))
-            whole += [
-                jnp.where(near, left[rim_rows], piece[:depth]),
-                piece[depth : wide - depth],
-                jnp.where(near, piece[wide - depth :], right[rim_rows]),
-            ]
-        cells[:, :lanes] = jnp.concatenate(whole, axis=0).astype(bf16)
-        second_out = network(False)
-        second_denoised = low[1] * moved[...] + low[2] * second_out
-        hand_over(cells[:, lanes:].astype(f32) + second_denoised)
-        for edge in edges:
-            edge.wait_send()
-
-    def unpick(base):
-        i = lax.broadcasted_iota(jnp.int32, (wide, cols), 0)
-        j = lax.broadcasted_iota(jnp.int32, (wide, cols), 1)
-        middle = (i >= HALO) & (i < wide - HALO)
-        return [
-            jnp.where(middle & (j == 2 * (base + i) + parity), 1.0, 0.0) for parity in range(2)
-        ]
+        second_out = network(False, wide)
+        fresh = jnp.concatenate(trimmed(moved, broad, HALO), axis=0)
+        second_denoised = low[1] * fresh + low[2] * second_out
+        given_t[rows_in] = cells[rows_in, lanes:].astype(f32) + second_denoised
+        hand_over(trimmed(given_t, wide, HALO))
 
     back = jnp.concatenate(
-        [piece for k in range(n_lat) for piece in unpick(k * own - HALO)], axis=0
+        [pick(k * own, own, parity) for k in range(n_lat) for parity in range(2)], axis=0
     ).astype(bf16)
     a = lax.broadcasted_iota(jnp.int32, (lanes, lanes), 0)
     b = lax.broadcasted_iota(jnp.int32, (lanes, lanes), 1)
     eye = jnp.where(a == b, 1.0, 0.0).astype(bf16)
     for k in range(n_lat):
         swap(k, k).wait_recv()
-    gathered = arrived[...].reshape(n_lat * 2 * wide, lanes)
+    gathered = arrived[...].reshape(cols, lanes)
     result = dot(dot_nt(eye, gathered).astype(bf16), back)[:used]
     out[0] = result.reshape(variables, rows, cols).astype(bf16)
     for k in range(n_lat):
@@ -534,11 +488,12 @@
     c0, c1 = expand.shape[1:]
     pairs = rows // 2
     total = n_lat * pairs
-    wide = cols // 2 // n_lat + 2 * HALO
+    own = cols // 2 // n_lat
+    wide = own + 2 * RIM
     slab = -(-wide // 16) * 16
     used = variables * rows
     lanes = -(-used // 128) * 128
-    depth = 4 * HALO
+    depth = 2 * RIM
     assert 2 * c0 == c1 and wide % 8 == 0 and n_lat % 2 == 0 and rows % 2 == 0
     split = (1, 3, 3, c0, c0)
     head_t = jnp.swapaxes(head, 1, 2)
@@ -560,8 +515,7 @@
         pltpu.VMEM((n_lat, 2 * wide, 2 * lanes), bf16),
         pltpu.VMEM((2, depth, 2 * lanes), bf16),
         pltpu.VMEM((2, n_lat, depth, 2 * lanes), bf16),
-        pltpu.VMEM((2, n_lat * depth, lanes), bf16),
-        pltpu.VMEM((2, n_lat * depth, lanes), bf16),
+        pltpu.VMEM((n_lat * 2 * wide, lanes), f32),
         pltpu.VMEM((n_lat * 2 * wide, lanes), f32),
         pltpu.VMEM((n_lat * 2 * wide, lanes), f32),
         pltpu.VMEM((1, 2 * c0), f32),
@@ -572,16 +526,14 @@
         pltpu.VMEM((3, total + 2, slab, c1), bf16),
         pltpu.VMEM((3, total + 2, 2 * wide, 2 * c0), bf16),
         pltpu.VMEM((total, 2 * wide, 2 * c0), bf16),
-        pltpu.VMEM((n_lat, 2 * wide, lanes), bf16),
-        pltpu.VMEM((n_lat, 2 * wide, lanes), bf16),
+        pltpu.VMEM((n_lat, 2 * own, lanes), bf16),
+        pltpu.VMEM((n_lat, 2 * own, lanes), bf16),
         pltpu.SemaphoreType.DMA((7,)),
         pltpu.SemaphoreType.DMA((6,)),
         pltpu.SemaphoreType.DMA((n_lat - 1,)),
         pltpu.SemaphoreType.DMA((n_lat - 1,)),
         pltpu.SemaphoreType.DMA((2,)),
         pltpu.SemaphoreType.DMA((2, n_lat)),
-        pltpu.SemaphoreType.DMA((2,)),
-        pltpu.SemaphoreType.DMA((2,)),
         pltpu.SemaphoreType.DMA((n_lat,)),
         pltpu.SemaphoreType.DMA((n_lat,)),
     ]

time: 34.8 us -> 32.3 us (0.928)
  Pallas kernels: 33.2 us -> 30.7 us
    pallas_call x1, Pallas kernels: 33.2 us -> 30.7 us  [on_device(): pl.pallas_call(functools.partial(kernel, n_lat, n_lon), out_shape=jax.Sha...]
where the time goes in v6:
time: 32.3 us; the launch traced here: 32.1 us
  Pallas kernels  30.7 us (95%)
  local copies, waits for them, and re-layouts  1.42 us (4%)
    pallas_call x1, Pallas kernels, on_device(): pl.pallas_call(functools.partial(kernel, n_lat, n_lon), out_shape=jax.Sha...  30.7 us
    unnamed x1, local copies, waits for them, and re-layouts  1.42 us

profile of v6, /device:TPU:0, one launch (start us, length us, event | category | flops | bytes accessed | tf_op | source)
XLA Modules:
  0.0 32.1 jit_solution(1343074445524221374)
XLA Ops:
  0.0 30.7 %shard_map.109 = bf16[1,12,8,256]{3,2,1,0:T(8,128)(2,1)} custom-call(bf16[1,12,8,256]{3,2,1,0:T(8,128)(2,1)} %start_hbm.1, bf16[12,8,256]{2,1,0:T(8,128)(2,1)} %prior_hbm.1, bf16[1,24,128]{2,1,0:T(8,128)(2,1)} %lift_w_hbm.1, f32[1,128]{1,0:T(1,128)} %gain_hbm.1, bf16[1,3,3,128,128]{4,3,2,1,0:T(8,128)(2,1)} %bitcast.3, bf16[1,128,256]{2,1,0:T(8,128)(2,1)} %expand_hbm.1, ...), custom_call_target="tpu_custom_call" | custom-call | tf_op jit(solution)/shard_map/pallas_call | solution.py:540
  30.7 1.4 %copy.13 = bf16[1,12,8,256]{3,2,1,0:T(8,128)(2,1)} copy(bf16[1,12,8,256]{3,2,1,0:T(8,128)(2,1)} %shard_map.109) | data formatting | bytes 98304

commit v7 on v6

--- a/solution.py
+++ b/solution.py
@@ -341,11 +341,15 @@
                 keep_fine(
                     lifted, k * pairs + p + 1, value[2 * wide * k : 2 * wide * (k + 1)]
                 )
-        if loading:
-            copies[0].wait()
-            copies[1].wait()
-        for group in groups(pairs):
-            acc = dot(stacked(fine, lifted, group), w0a[...].reshape(12 * c0, 2 * c0))
+        def loaded(*which):
+            if loading:
+                for n in which:
+                    copies[n].wait()
+
+        def down(group):
+            return dot(stacked(fine, lifted, group), w0a[...].reshape(12 * c0, 2 * c0))
+
+        def after_down(group, acc):
             value = silu(acc).astype(bf16)
             pooled = []
             for k, index in enumerate(group):
@@ -359,23 +363,25 @@
             result = dot(jnp.concatenate(pooled, axis=0).astype(bf16), expand_w)
             for k, index in enumerate(group):
                 keep_coarse(widened, index + 1, result[slab * k : slab * (k + 1)])
-        if loading:
-            copies[2].wait()
-        for group in groups(2 * pairs):
-            acc = dot(
+
+        def coarse_a(group):
+            return dot(
                 stacked(coarse_window, widened, group),
                 w1a[...].reshape(9 * w1a.shape[1], w1a.shape[2]),
             )
+
+        def after_coarse_a(group, acc):
             value = silu(acc)
             for k, index in enumerate(group):
                 keep_coarse(inner, index + 1, value[slab * k : slab * (k + 1)])
-        if loading:
-            copies[3].wait()
-        for group in groups(2 * pairs):
-            acc = dot(
+
+        def coarse_b(group):
+            return dot(
                 stacked(coarse_window, inner, group),
                 w1b[...].reshape(9 * w1b.shape[1], w1b.shape[2]),
             )
+
+        def after_coarse_b(group, acc):
             skip = jnp.concatenate([widened[1, index + 1] for index in group], axis=0)
             projected = dot((silu(acc) + skip.astype(f32)).astype(bf16), shrink_w)
             for k, index in enumerate(group):
@@ -385,14 +391,34 @@
                     index + 1,
                     jnp.concatenate([piece, piece], axis=0) + first[index, 0:tall].astype(f32),
                 )
-        if loading:
-            copies[4].wait()
-            copies[5].wait()
-        for group in groups(pairs):
-            acc = dot(stacked(fine, merged, group), w0b[...].reshape(12 * c0, 2 * c0))
+
+        def up(group):
+            return dot(stacked(fine, merged, group), w0b[...].reshape(12 * c0, 2 * c0))
+
+        def after_up(group, acc):
             value = silu(acc).astype(bf16)
             for k, index in enumerate(group):
                 last[index, 0:tall] = value[2 * wide * k : 2 * wide * (k + 1)]
+
+        middle = total // 2
+        tasks = [(down, after_down, group, (0, 1)) for group in groups(pairs)]
+        tasks += [(coarse_a, after_coarse_a, group, (2,)) for group in groups(middle)]
+        tasks += [
+            (coarse_b, after_coarse_b, group, (3,))
+            for group in (range(middle - 1), range(middle - 1, total))
+        ]
+        tasks += [(up, after_up, group, (4, 5)) for group in groups(pairs)]
+        waited = set()
+        pending = None
+        for ahead, behind, group, weights in tasks:
+            if weights not in waited:
+                waited.add(weights)
+                loaded(*weights)
+            acc = ahead(group)
+            if pending is not None:
+                pending()
+            pending = functools.partial(behind, group, acc)
+        pending()
         return dot(
             jnp.concatenate(
                 [
@@ -494,7 +520,8 @@
     used = variables * rows
     lanes = -(-used // 128) * 128
     depth = 2 * RIM
-    assert 2 * c0 == c1 and wide % 8 == 0 and n_lat % 2 == 0 and rows % 2 == 0
+    assert total // 2 < total - pairs and pairs < total // 2 - 1
+    assert 2 * c0 == c1 and wide % 8 == 0 and n_lat % 4 == 0 and rows % 4 == 0
     split = (1, 3, 3, c0, c0)
     head_t = jnp.swapaxes(head, 1, 2)
     scratch = [

time: 32.3 us -> 27.9 us (0.86)
  Pallas kernels: 30.7 us -> 26.3 us
    pallas_call x1, Pallas kernels: 30.7 us -> 26.3 us  [on_device(): pl.pallas_call(functools.partial(kernel, n_lat, n_lon), out_shape=jax.Sha...]
where the time goes in v7:
time: 27.9 us; the launch traced here: 27.7 us
  Pallas kernels  26.3 us (94%)
  local copies, waits for them, and re-layouts  1.42 us (5%)
    pallas_call x1, Pallas kernels, on_device(): pl.pallas_call(functools.partial(kernel, n_lat, n_lon), out_shape=jax.Sha...  26.3 us
    unnamed x1, local copies, waits for them, and re-layouts  1.42 us

profile of v7, /device:TPU:0, one launch (start us, length us, event | category | flops | bytes accessed | tf_op | source)
XLA Modules:
  0.0 27.7 jit_solution(11076199613901730782)
XLA Ops:
  0.0 26.3 %shard_map.109 = bf16[1,12,8,256]{3,2,1,0:T(8,128)(2,1)} custom-call(bf16[1,12,8,256]{3,2,1,0:T(8,128)(2,1)} %start_hbm.1, bf16[12,8,256]{2,1,0:T(8,128)(2,1)} %prior_hbm.1, bf16[1,24,128]{2,1,0:T(8,128)(2,1)} %lift_w_hbm.1, f32[1,128]{1,0:T(1,128)} %gain_hbm.1, bf16[1,3,3,128,128]{4,3,2,1,0:T(8,128)(2,1)} %bitcast.3, bf16[1,128,256]{2,1,0:T(8,128)(2,1)} %expand_hbm.1, ...), custom_call_target="tpu_custom_call" | custom-call | tf_op jit(solution)/shard_map/pallas_call | solution.py:567
  26.3 1.4 %copy.13 = bf16[1,12,8,256]{3,2,1,0:T(8,128)(2,1)} copy(bf16[1,12,8,256]{3,2,1,0:T(8,128)(2,1)} %shard_map.109) | data formatting | bytes 98304
